TPU v7x, 512 devices: a whole 4x4x16 slice. The times are simulated.
512 devices in a mesh: lat: 64 (over z, x_lo, core), tok: 8 (over x_hi, y).
Axes of the slice: x: 4 (x_hi: 2, x_lo: 2; x = x_hi * 2 + x_lo), y: 4, z: 16, core: 2. Of those that a mesh axis runs over, the one named last changes fastest.
Arguments:
- inputs: bfloat16 [512, 4096], P('lat', 'tok'), may hold values from -6 to 6
- targets: bfloat16 [512, 4096], P('lat', 'tok'), may hold values from -24 to 24
- enc_weight: bfloat16 [4096, 65536], P('tok', 'lat'), may hold values from -0.09375 to 0.09375
- enc_bias: float32 [65536], P('lat'), may hold values from -3 to 3
- dec_weight: bfloat16 [65536, 4096], P('lat', 'tok'), may hold values from -0.0234375 to 0.0234375
- dec_bias: float32 [4096], P('tok'), may hold values from -3 to 3
Outputs:
- loss: float32 [], replicated
- grad_enc: bfloat16 [4096, 65536], P('tok', 'lat')
- grad_dec: bfloat16 [65536, 4096], P('lat', 'tok')
- grad_enc_bias: float32 [65536], P('lat')
- grad_dec_bias: float32 [4096], P('tok')
All inputs are finite; a program needn't handle non-finite values.
Results may differ from a plain program's by a relative error of at most 0.04.
Values may be sent and summed in bfloat16 or wider, within the bound.
No kernel may reach another device: no remote copies, remote signals or barrier semaphores. Data moves between devices by JAX's collectives and lax.ppermute only.
A program may use at most 64 MiB of HBM per device.

v0:
```python
import math

import jax
import jax.numpy as jnp
from jax import lax
from jax.sharding import PartitionSpec as P

sparsity = 0.03


def local(inputs, targets, enc_weight, enc_bias, dec_weight, dec_bias):
    row_count = inputs.shape[0]
    cycle_size = lax.axis_size("lat")
    total_rows = row_count * cycle_size
    full_width = inputs.shape[1] * lax.axis_size("tok")
    scale_root = math.sqrt(total_rows)
    every_row = lax.all_gather(inputs, "lat", axis=0, tiled=True)
    partial_value = jnp.dot(every_row, enc_weight, preferred_element_type=jnp.float32)
    preact = lax.psum(partial_value.astype(jnp.bfloat16), "tok").astype(jnp.float32) + enc_bias
    lifted = jnp.maximum(preact, 0.0)
    latent = lifted * lifted
    latent_low = latent.astype(jnp.bfloat16)
    recon = (
        lax.psum_scatter(
            jnp.dot(latent_low, dec_weight, preferred_element_type=jnp.float32),
            "lat",
            scatter_dimension=0,
            tiled=True,
        )
        + dec_bias
    )
    residual = recon - targets.astype(jnp.float32)
    local_loss = 0.5 * jnp.sum(residual * residual) + sparsity * jnp.sum(latent) / lax.axis_size(
        "tok"
    )
    grad_recon = (residual / scale_root).astype(jnp.bfloat16)
    column_part = jnp.sum(grad_recon.astype(jnp.float32), axis=0)
    column_rows, loss_rows = (
        lax.all_gather(column_part.reshape(1, -1), "lat", axis=0, tiled=True),
        lax.all_gather(local_loss.reshape(1), "lat", axis=0, tiled=True),
    )
    grad_dec_bias = jnp.sum(column_rows, axis=0)
    lat_loss = jnp.sum(loss_rows)
    block_losses = lax.all_gather(lat_loss.reshape(1), "tok", axis=0, tiled=True)
    loss = jnp.sum(block_losses) / (total_rows * full_width)
    every_grad = lax.all_gather(grad_recon, "lat", axis=0, tiled=True)
    back_part = lax.dot_general(
        every_grad, dec_weight, (((1,), (1,)), ((), ())), preferred_element_type=jnp.float32
    )
    back_grad = (
        lax.psum(back_part.astype(jnp.bfloat16), "tok").astype(jnp.float32) + sparsity / scale_root
    )
    grad_pre = back_grad * (2.0 * lifted)
    grad_enc_bias = jnp.sum(grad_pre, axis=0)
    grad_enc = lax.dot_general(
        every_row,
        grad_pre.astype(jnp.bfloat16),
        (((0,), (0,)), ((), ())),
        preferred_element_type=jnp.float32,
    ).astype(jnp.bfloat16)
    grad_dec = lax.dot_general(
        latent_low, every_grad, (((0,), (0,)), ((), ())), preferred_element_type=jnp.float32
    ).astype(jnp.bfloat16)
    return (loss, grad_enc, grad_dec, grad_enc_bias, grad_dec_bias)


def solution(mesh):
    in_specs = (
        P("lat", "tok"),
        P("lat", "tok"),
        P("tok", "lat"),
        P("lat"),
        P("lat", "tok"),
        P("tok"),
    )
    out_specs = (P(), P("tok", "lat"), P("lat", "tok"), P("lat"), P("tok"))
    return jax.shard_map(local, mesh=mesh, in_specs=in_specs, out_specs=out_specs, check_vma=False)
```

profile of v0, /device:TPU:8, one launch (start us, length us, event | category | flops | bytes accessed | tf_op | source)
XLA Modules:
  0.0 718.6 jit_solution(11070728825704635531)
XLA Ops:
  7.2 0.0 copy-start
  7.2 0.0 all-reduce.5.cloned.1.call-start
  7.2 71.6 %all_gather.15 = bf16[512,512]{1,0:T(8,128)(2,1)S(1)} all-gather(bf16[8,512]{1,0:T(8,128)(2,1)} %param.6), channel_id=1, replica_groups=mesh['lat'=64,'tok'=8] {'lat'}, dimensions={0}, use_global_device_ids=true | all-gather | bytes 532480 | tf_op jit(solution)/shard_map/all_gather | solution.py:17
  78.8 0.0 copy-start.3
  78.8 0.8 copy-done.3
  79.6 2.9 convolution_convert_fusion.3
  82.5 0.0 copy-start.5
  82.5 0.0 all-reduce.5.cloned.1.call-update
  82.5 0.0 reduce-scatter.2.cloned.1.call-start
  82.6 94.8 %all-reduce.5.cloned.1.call-done = bf16[512,1024]{1,0:T(8,128)(2,1)} async-done(((bf16[512,1024]{1,0:T(8,128)(2,1)}), bf16[512,1024]{1,0:T(8,128)(2,1)}) %all-reduce.5.cloned.1.call-update) | async-done | bytes 1048592 | tf_op jit(solution)/shard_map/psum | solution.py:19
  177.4 0.0 copy-done
  177.4 0.0 copy-done.5
  177.4 2.9 fusion.12
  180.3 0.0 copy-start.4
  180.3 0.0 copy-start.6
  180.3 0.0 reduce-scatter.2.cloned.1.call-update
  180.3 0.0 all-reduce.7.cloned.1.call-start
  180.4 228.2 %reduce-scatter.2.cloned.1.call-done = f32[8,512]{1,0:T(8,128)} async-done(((f32[512,512]{1,0:T(8,128)}), f32[8,512]{1,0:T(8,128)}) %reduce-scatter.2.cloned.1.call-update) | async-done | bytes 16400 | tf_op jit(solution)/shard_map/reduce_scatter | solution.py:24
  408.6 0.0 copy-done.4
  408.6 0.0 copy-done.6
  408.6 1.3 convert_reduce_fusion
  410.0 60.6 %all_gather.18 = bf16[512,512]{1,0:T(8,128)(2,1)S(1)} all-gather(bf16[8,512]{1,0:T(8,128)(2,1)S(1)} %get-tuple-element.18), channel_id=1, replica_groups=mesh['lat'=64,'tok'=8] {'lat'}, dimensions={0}, use_global_device_ids=true | all-gather | bytes 532480 | tf_op jit(solution)/shard_map/all_gather | solution.py:46
  470.6 1.7 convolution_convert_fusion.2
  472.3 0.0 copy-start.1
  472.3 0.0 all-reduce.7.cloned.1.call-update
  472.4 1.4 dynamic-slice
  473.7 1.3 dynamic-slice.1
  475.6 61.6 %all-gather.1 = f32[64,1,512]{2,1,0:T(1,128)S(1)} all-gather(f32[1,1,512]{2,1,0:T(1,128)S(1)} %bitcast.14), channel_id=2, replica_groups=mesh['lat'=64,'tok'=8] {'lat'}, dimensions={0}, use_global_device_ids=true | all-gather | bytes 133120 | tf_op jit(solution)/shard_map/all_gather | solution.py:39
  537.2 0.0 copy-done.1
  537.2 1.7 convolution_convert_fusion
  538.9 31.5 %all-reduce.7.cloned.1.call-done = bf16[512,1024]{1,0:T(8,128)(2,1)} async-done(((bf16[512,1024]{1,0:T(8,128)(2,1)}), bf16[512,1024]{1,0:T(8,128)(2,1)}) %all-reduce.7.cloned.1.call-update) | async-done | bytes 1048592 | tf_op jit(solution)/shard_map/psum | solution.py:51
  570.4 0.0 copy-start.2
  570.4 2.6 fusion.3
  573.7 0.8 dynamic-update-slice
  574.4 104.7 %all-reduce = f32[64]{0:T(128)S(1)} all-reduce(f32[64]{0:T(128)S(1)} %dynamic-update-slice), channel_id=1, replica_groups=mesh['lat'=64,'tok'=8] {'lat'}, use_global_device_ids=true, to_apply=%add | all-reduce | flops 64 | bytes 512
  679.1 0.6 reduce_sum.65
  679.7 1.4 dynamic-update-slice.1
  681.1 0.7 reduce_sum.69
  681.8 22.9 %all-reduce.1 = f32[8]{0:T(128)S(1)} all-reduce(f32[8]{0:T(128)S(1)} %dynamic-update-slice.1), channel_id=1, replica_groups=mesh['lat'=64,'tok'=8] {'tok'}, use_global_device_ids=true, to_apply=%add.1 | all-reduce | flops 8 | bytes 64
  704.6 0.6 reduce_sum.66
  705.2 0.0 copy-done.2
  705.2 2.8 fusion.5
  708.0 2.3 copy.12
  (2 shorter events, 0.0 us)
Async XLA Ops:
  7.2 170.2 %copy-start = (bf16[1024,512]{1,0:T(8,128)(2,1)S(1)}, bf16[1024,512]{1,0:T(8,128)(2,1)}, u32[]{:S(2)}) copy-start(bf16[1024,512]{1,0:T(8,128)(2,1)} %param.10) | copy-start | bytes 3145732
  7.2 170.2 %all-reduce.5.cloned.1.call-start = ((), (), s32[]{:S(2)}) async-start(), calls=%async_computation.1 | async-start | bytes 2097152 | tf_op jit(solution)/shard_map/psum | solution.py:19
  78.8 0.8 copy-start.3
  82.5 94.9 %copy-start.5 = (f32[1024]{0:T(1024)S(1)}, f32[1024]{0:T(1024)}, u32[]{:S(2)}) copy-start(f32[1024]{0:T(1024)} %param.9) | copy-start | bytes 12292
  82.5 326.1 %reduce-scatter.2.cloned.1.call-start = ((), (), s32[]{:S(2)}) async-start(), calls=%async_computation.2 | async-start | bytes 1064960 | tf_op jit(solution)/shard_map/reduce_scatter | solution.py:24
  180.3 228.3 %copy-start.4 = (bf16[8,512]{1,0:T(8,128)(2,1)S(1)}, bf16[8,512]{1,0:T(8,128)(2,1)}, u32[]{:S(2)}) copy-start(bf16[8,512]{1,0:T(8,128)(2,1)} %param.7) | copy-start | bytes 24580
  180.3 228.3 %copy-start.6 = (f32[512]{0:T(512)S(1)}, f32[512]{0:T(512)}, u32[]{:S(2)}) copy-start(f32[512]{0:T(512)} %param.11) | copy-start | bytes 6148
  180.3 390.0 %all-reduce.7.cloned.1.call-start = ((), (), s32[]{:S(2)}) async-start(), calls=%async_computation.3 | async-start | bytes 2097152 | tf_op jit(solution)/shard_map/psum | solution.py:51
  472.3 64.9 %copy-start.1 = (bf16[512,1024]{1,0:T(8,128)(2,1)S(1)}, bf16[512,1024]{1,0:T(8,128)(2,1)}, u32[]{:S(2)}) copy-start(bf16[512,1024]{1,0:T(8,128)(2,1)} %all-reduce.5.cloned.1.call-done) | copy-start | bytes 3145732
  570.4 134.8 %copy-start.2 = (bf16[512,1024]{1,0:T(8,128)(2,1)S(1)}, bf16[512,1024]{1,0:T(8,128)(2,1)}, u32[]{:S(2)}) copy-start(bf16[512,1024]{1,0:T(8,128)(2,1)} %all-reduce.7.cloned.1.call-done) | copy-start | bytes 3145732
Sparse Core Ops, SparseCore 0:
  82.6 94.7 all-reduce.4
  180.8 227.8 reduce-scatter.1
  472.5 97.8 all-reduce.6
where the time goes:
time: 719 us
  waiting for transfers between devices  355 us (49%)
  blocking collectives  321 us (45%)
  between operations  16.9 us (2%)
  matrix products  12.1 us (2%)
  local copies, waits for them, and re-layouts  7.84 us (1%)
    reduce_scatter x1, waiting for transfers between devices, local(): lax.psum_scatter(jnp.dot(latent_low, dec_weight, preferred_element_type=j...  228 us
    unnamed x2, blocking collectives  128 us
    psum x1, waiting for transfers between devices, local(): lax.psum(partial_value.astype(jnp.bfloat16), 'tok').astype(jnp.float32)  94.8 us
    all_gather x1, blocking collectives, local(): every_row = lax.all_gather(inputs, 'lat', axis=0, tiled=True)  71.6 us
    all_gather x1, blocking collectives, local(): lax.all_gather(column_part.reshape(1, -1), 'lat', axis=0, tiled=True)  61.6 us
    all_gather x1, blocking collectives, local(): every_grad = lax.all_gather(grad_recon, 'lat', axis=0, tiled=True)  60.6 us
    psum x1, waiting for transfers between devices, local(): lax.psum(back_part.astype(jnp.bfloat16), 'tok').astype(jnp.float32)  31.5 us
  transfers between devices with their start and end apart: 3, of which 3 were waited for; matrix products, arithmetic and copies ran while one was open for 1% of the time, Pallas kernels for 0%

commit v1 on v0

v1 whole, which is shorter than its diff:
```python
import math

import jax
import jax.numpy as jnp
from jax import lax
from jax.sharding import Mesh, PartitionSpec as P

sparsity = 0.03

Z, XL, C, XH, Y = 16, 2, 2, 2, 4
LAT = ("z", "xl", "c")
TOK = ("xh", "y")
N_TOK = XH * Y
bf16, f32 = jnp.bfloat16, jnp.float32


def dot(a, b, da, db):
    return lax.dot_general(a, b, (((da,), (db,)), ((), ())), preferred_element_type=f32)


def share(x, axes, n):
    copies = jnp.broadcast_to(x[None], (n,) + x.shape).reshape(n * x.shape[0], x.shape[1])
    return lax.all_to_all(copies, axes, 0, 0, tiled=True)


def gather_lat(x):
    x = share(x, "z", Z)
    x = lax.all_gather(x, "xl", axis=0, tiled=True)
    return lax.all_gather(x, "c", axis=0, tiled=True)


def halve(x, axis):
    half = x.shape[0] // 2
    me = lax.axis_index(axis)
    send = lax.dynamic_slice_in_dim(x, (1 - me) * half, half, 0).astype(bf16)
    keep = lax.dynamic_slice_in_dim(x, me * half, half, 0)
    both = lax.all_gather(send, axis, axis=0, tiled=False)
    return keep + lax.dynamic_index_in_dim(both, 1 - me, 0, keepdims=False).astype(f32)


def scatter_lat(x):
    x = halve(x, "c")
    x = halve(x, "xl")
    parts = lax.all_to_all(x.astype(bf16), "z", 0, 0, tiled=True)
    return jnp.sum(parts.reshape(Z, -1, x.shape[1]).astype(f32), axis=0)


def scatter_tok(x):
    parts = lax.all_to_all(x, TOK, 0, 0, tiled=True)
    return parts.reshape(N_TOK, -1, x.shape[1])


def split2(v):
    high = v.astype(bf16)
    return high, (v - high.astype(f32)).astype(bf16)


def local(inputs, targets, enc_weight, enc_bias, dec_weight, dec_bias):
    rows, width = inputs.shape
    total_rows = rows * Z * XL * C
    full_width = width * N_TOK
    scale_root = math.sqrt(total_rows)

    every_row = gather_lat(inputs)
    pre = dot(every_row, enc_weight, 1, 0).astype(bf16)
    preact = jnp.sum(scatter_tok(pre).astype(f32), axis=0) + enc_bias
    lifted = jnp.maximum(preact, 0.0)
    latent = lifted * lifted
    latent_sum = jnp.sum(latent)
    latent_low = share(latent.astype(bf16), TOK, N_TOK)

    recon = scatter_lat(dot(latent_low, dec_weight, 1, 0)) + dec_bias
    residual = recon - targets.astype(f32)
    grad_recon = (residual / scale_root).astype(bf16)
    row_loss = 0.5 * jnp.sum(residual * residual, axis=1, keepdims=True) + (
        sparsity / rows
    ) * latent_sum
    high, low = split2(row_loss)
    lane = lax.broadcasted_iota(jnp.int32, (rows, 128), 1)
    zero = jnp.zeros((rows, 128), bf16)
    extra = jnp.where(lane == 0, high, jnp.where(lane == 1, low, zero))
    gathered = gather_lat(jnp.concatenate([grad_recon, extra], axis=1))
    every_grad = gathered[:, :width]
    lat_loss = jnp.sum(gathered[:, width:].astype(f32))
    grad_dec_bias = jnp.sum(every_grad.astype(f32), axis=0)

    back = dot(every_grad, dec_weight, 1, 1).astype(bf16)
    back_grad = jnp.sum(scatter_tok(back).astype(f32), axis=0) + sparsity / scale_root
    grad_pre = back_grad * (2.0 * lifted)
    grad_dec = dot(latent_low, every_grad, 0, 0).astype(bf16)

    lats = grad_pre.shape[1]
    high, low = split2(lat_loss)
    bias_high, bias_low = split2(jnp.sum(grad_pre, axis=0, keepdims=True))
    row = lax.broadcasted_iota(jnp.int32, (8, lats), 0)
    zero = jnp.zeros((8, lats), bf16)
    tail = jnp.where(row == 0, bias_high, jnp.where(row == 1, bias_low, zero))
    tail = jnp.where(row == 2, high, jnp.where(row == 3, low, tail))
    shared = share(
        jnp.concatenate([grad_pre.astype(bf16), tail], axis=0), TOK, N_TOK
    ).reshape(N_TOK, -1, lats)
    part = shared.shape[1] - 8
    grad_pre_low = shared[:, :part].reshape(-1, lats)
    tails = jnp.sum(shared[:, part:].astype(f32), axis=0)
    grad_enc_bias = tails[0] + tails[1]
    loss = (tails[2, 0] + tails[3, 0]) / (total_rows * full_width)
    grad_enc = dot(every_row, grad_pre_low, 0, 0).astype(bf16)
    return (loss, grad_enc, grad_dec, grad_enc_bias, grad_dec_bias)


def solution(mesh):
    fine = Mesh(mesh.devices.reshape(Z, XL, C, XH, Y), LAT + TOK)
    in_specs = (
        P(LAT, TOK),
        P(LAT, TOK),
        P(TOK, LAT),
        P(LAT),
        P(LAT, TOK),
        P(TOK),
    )
    out_specs = (P(), P(TOK, LAT), P(LAT, TOK), P(LAT), P(TOK))
    return jax.shard_map(local, mesh=fine, in_specs=in_specs, out_specs=out_specs, check_vma=False)
```

time: 719 us -> 190 us (0.26)
  waiting for transfers between devices: 355 us -> 52.4 us
  blocking collectives: 321 us -> 95.3 us
  starting transfers between devices: 0.12 us -> 19.8 us
  between operations: 16.9 us -> 5.22 us
    reduce_scatter x1 -> x0, waiting for transfers between devices: 228 us -> none  [local(): lax.psum_scatter(jnp.dot(latent_low, dec_weight, preferred_element_type=j...]
    all_gather x3 -> x6, blocking collectives: 194 us -> 24.4 us  [the longest x2 11.6 us: gather_lat(): x = lax.all_gather(x, 'xl', axis=0, tiled=True)]
    unnamed x2 -> x0, blocking collectives: 128 us -> none
    psum x2 -> x0, waiting for transfers between devices: 126 us -> none  [the longest x1 94.8 us: local(): lax.psum(partial_value.astype(jnp.bfloat16), 'tok').astype(jnp.float32)]
    all_to_all x0 -> x3, blocking collectives: none -> 70.8 us  [the longest x2 48 us: share(): return lax.all_to_all(copies, axes, 0, 0, tiled=True)]
    all_to_all x0 -> x4, waiting for transfers between devices: none -> 52.4 us  [the longest x2 26 us: share(): return lax.all_to_all(copies, axes, 0, 0, tiled=True)]
    all_to_all x0 -> x4, starting transfers between devices: none -> 19.8 us  [the longest x2 10.6 us: share(): return lax.all_to_all(copies, axes, 0, 0, tiled=True)]
  transfers between devices with their start and end apart: 3 -> 4, of which waited for: 3 -> 4; matrix products, arithmetic and copies ran while one was open for 1% -> 2% of each run, Pallas kernels for 0% -> 0%
where the time goes in v1:
time: 190 us; the launch traced here: 189 us
  blocking collectives  95.3 us (50%)
  waiting for transfers between devices  52.4 us (28%)
  starting transfers between devices  19.8 us (10%)
  matrix products  6.81 us (4%)
  local copies, waits for them, and re-layouts  5.82 us (3%)
  between operations  5.22 us (3%)
  other arithmetic  4.16 us (2%)
    all_to_all x2, blocking collectives, share(): return lax.all_to_all(copies, axes, 0, 0, tiled=True)  48 us
    all_to_all x2, waiting for transfers between devices, share(): return lax.all_to_all(copies, axes, 0, 0, tiled=True)  26 us
    all_to_all x1, blocking collectives, scatter_tok(): parts = lax.all_to_all(x, TOK, 0, 0, tiled=True)  22.8 us
    all_to_all x1, waiting for transfers between devices, scatter_lat(): parts = lax.all_to_all(x.astype(bf16), 'z', 0, 0, tiled=True)  13.5 us
    all_to_all x1, waiting for transfers between devices, scatter_tok(): parts = lax.all_to_all(x, TOK, 0, 0, tiled=True)  12.9 us
    all_gather x2, blocking collectives, gather_lat(): x = lax.all_gather(x, 'xl', axis=0, tiled=True)  11.6 us
    all_to_all x2, starting transfers between devices, share(): return lax.all_to_all(copies, axes, 0, 0, tiled=True)  10.6 us
    all_gather x2, blocking collectives, halve(): both = lax.all_gather(send, axis, axis=0, tiled=False)  8.4 us
  transfers between devices with their start and end apart: 4, of which 4 were waited for; matrix products, arithmetic and copies ran while one was open for 2% of the time, Pallas kernels for 0%

profile of v1, /device:TPU:8, one launch (start us, length us, event | category | flops | bytes accessed | tf_op | source)
XLA Modules:
  0.0 189.5 jit_solution(1657190173287120173)
XLA Ops:
  0.6 0.0 copy-start
  0.6 0.0 copy-start.7
  0.7 0.9 broadcast_in_dim.67
  1.5 29.7 %all_to_all.60 = bf16[16,8,512]{2,1,0:T(8,128)(2,1)S(1)} all-to-all(bf16[16,8,512]{2,1,0:T(8,128)(2,1)S(1)} %broadcast_in_dim.67), channel_id=1, replica_groups=mesh['z'=16,'xl'=2,'c'=2,'xh'=2,'y'=4] {'z'}, dimensions={0} | all-to-all | bytes 262144 | tf_op jit(solution)/shard_map/all_to_all | solution.py:23
  31.2 5.6 %all_gather.24 = bf16[256,512]{1,0:T(8,128)(2,1)S(1)} all-gather(bf16[128,512]{1,0:T(8,128)(2,1)S(1)} %bitcast.36), channel_id=1, replica_groups=mesh['z'=16,'xl'=2,'c'=2,'xh'=2,'y'=4] {'xl'}, dimensions={0}, use_global_device_ids=true | all-gather | bytes 393216 | tf_op jit(solution)/shard_map/all_gather | solution.py:28
  36.8 2.2 %all_gather.25 = bf16[512,512]{1,0:T(8,128)(2,1)S(1)} all-gather(bf16[256,512]{1,0:T(8,128)(2,1)S(1)} %all_gather.24), channel_id=1, replica_groups=mesh['z'=16,'xl'=2,'c'=2,'xh'=2,'y'=4] {'c'}, dimensions={0}, use_global_device_ids=true | all-gather | bytes 786432 | tf_op jit(solution)/shard_map/all_gather | solution.py:29
  39.0 0.0 copy-done.7
  39.0 0.7 convolution_convert_fusion.3
  39.7 0.1 copy-done.2
  39.8 22.8 %all_to_all.61 = bf16[8,64,1024]{2,1,0:T(8,128)(2,1)S(1)} all-to-all(bf16[8,64,1024]{2,1,0:T(8,128)(2,1)S(1)} %bitcast.33), channel_id=1, replica_groups=mesh['z'=16,'xl'=2,'c'=2,'xh'=2,'y'=4] {'xh','y'}, dimensions={0} | all-to-all | bytes 2097152 | tf_op jit(solution)/shard_map/all_to_all | solution.py:49
  62.6 0.2 convert_reduce_fusion.1
  62.8 0.5 copy-done.4
  63.3 0.7 multiply_convert_fusion
  64.0 1.1 broadcast_in_dim.68
  65.1 5.3 %all-to-all-start.2 = ((bf16[8,64,1024]{2,1,0:T(8,128)(2,1)}), bf16[8,64,1024]{2,1,0:T(8,128)(2,1)S(1)}, u32[]{:S(2)}, u32[]{:S(2)}) async-start(bf16[8,64,1024]{2,1,0:T(8,128)(2,1)} %broadcast_in_dim.68), calls=%async_computation.2 | async-start | bytes 2097152 | tf_op jit(solution)/shard_map/all_to_all | solution.py:23
  70.4 13.5 %all-to-all-done.2 = bf16[8,64,1024]{2,1,0:T(8,128)(2,1)S(1)} async-done(((bf16[8,64,1024]{2,1,0:T(8,128)(2,1)}), bf16[8,64,1024]{2,1,0:T(8,128)(2,1)S(1)}, u32[]{:S(2)}, u32[]{:S(2)}) %all-to-all-start.2) | async-done | bytes 1048608 | tf_op jit(solution)/shard_map/all_to_all | solution.py:23
  83.8 0.0 copy-done
  83.8 0.7 fusion.9
  84.6 2.2 %all-gather = bf16[512,512]{1,0:T(8,128)(2,1)S(1)} all-gather(bf16[256,512]{1,0:T(8,128)(2,1)S(1)} %dynamic-slice_convert_fusion), channel_id=2, replica_groups=mesh['z'=16,'xl'=2,'c'=2,'xh'=2,'y'=4] {'c'}, dimensions={0}, use_global_device_ids=true | all-gather | bytes 786432 | tf_op jit(solution)/shard_map/all_gather | solution.py:37
  86.8 0.1 convert_add_fusion
  86.9 6.2 %all-gather.1 = bf16[256,512]{1,0:T(8,128)(2,1)S(1)} all-gather(bf16[128,512]{1,0:T(8,128)(2,1)S(1)} %dynamic-slice_convert_fusion.1), channel_id=3, replica_groups=mesh['z'=16,'xl'=2,'c'=2,'xh'=2,'y'=4] {'xl'}, dimensions={0}, use_global_device_ids=true | all-gather | bytes 393216 | tf_op jit(solution)/shard_map/all_gather | solution.py:37
  93.1 0.7 fusion.4
  93.8 0.0 copy-done.1
  93.8 3.8 %all-to-all-start.3 = ((bf16[16,8,512]{2,1,0:T(8,128)(2,1)}), bf16[16,8,512]{2,1,0:T(8,128)(2,1)S(1)}, u32[]{:S(2)}, u32[]{:S(2)}) async-start(bf16[16,8,512]{2,1,0:T(8,128)(2,1)} %fusion.4), calls=%async_computation.3 | async-start | bytes 262144 | tf_op jit(solution)/shard_map/all_to_all | solution.py:44
  98.3 13.5 %all-to-all-done.3 = bf16[16,8,512]{2,1,0:T(8,128)(2,1)S(1)} async-done(((bf16[16,8,512]{2,1,0:T(8,128)(2,1)}), bf16[16,8,512]{2,1,0:T(8,128)(2,1)S(1)}, u32[]{:S(2)}, u32[]{:S(2)}) %all-to-all-start.3) | async-done | bytes 131104 | tf_op jit(solution)/shard_map/all_to_all | solution.py:44
  111.8 0.0 copy-done.5
  111.8 0.1 multiply_convert_fusion.1
  111.9 0.1 select_select_fusion.1
  112.1 18.3 %all_to_all.62 = bf16[16,8,640]{2,1,0:T(8,128)(2,1)S(1)} all-to-all(bf16[16,8,640]{2,1,0:T(8,128)(2,1)S(1)} %broadcast_in_dim.72), channel_id=1, replica_groups=mesh['z'=16,'xl'=2,'c'=2,'xh'=2,'y'=4] {'z'}, dimensions={0} | all-to-all | bytes 327680 | tf_op jit(solution)/shard_map/all_to_all | solution.py:23
  130.4 6.0 %all_gather.30 = bf16[256,640]{1,0:T(8,128)(2,1)S(1)} all-gather(bf16[128,640]{1,0:T(8,128)(2,1)S(1)} %bitcast.34), channel_id=1, replica_groups=mesh['z'=16,'xl'=2,'c'=2,'xh'=2,'y'=4] {'xl'}, dimensions={0}, use_global_device_ids=true | all-gather | bytes 491520 | tf_op jit(solution)/shard_map/all_gather | solution.py:28
  136.4 2.3 %all_gather.31 = bf16[512,640]{1,0:T(8,128)(2,1)S(1)} all-gather(bf16[256,640]{1,0:T(8,128)(2,1)S(1)} %all_gather.30), channel_id=1, replica_groups=mesh['z'=16,'xl'=2,'c'=2,'xh'=2,'y'=4] {'c'}, dimensions={0}, use_global_device_ids=true | all-gather | bytes 983040 | tf_op jit(solution)/shard_map/all_gather | solution.py:29
  138.6 1.7 convolution_convert_fusion.2
  140.3 5.4 %all-to-all-start.5 = ((bf16[8,64,1024]{2,1,0:T(8,128)(2,1)}), bf16[8,64,1024]{2,1,0:T(8,128)(2,1)S(1)}, u32[]{:S(2)}, u32[]{:S(2)}) async-start(bf16[8,64,1024]{2,1,0:T(8,128)(2,1)} %bitcast.31), calls=%async_computation.5 | async-start | bytes 2097152 | tf_op jit(solution)/shard_map/all_to_all | solution.py:49
  145.7 0.7 convert_reduce_fusion.4
  147.7 12.9 %all-to-all-done.5 = bf16[8,64,1024]{2,1,0:T(8,128)(2,1)S(1)} async-done(((bf16[8,64,1024]{2,1,0:T(8,128)(2,1)}), bf16[8,64,1024]{2,1,0:T(8,128)(2,1)S(1)}, u32[]{:S(2)}, u32[]{:S(2)}) %all-to-all-start.5) | async-done | bytes 1048608 | tf_op jit(solution)/shard_map/all_to_all | solution.py:49
  160.6 0.2 convert_reduce_fusion
  160.8 0.1 fusion.6
  160.9 0.1 select_select_fusion
  161.0 1.2 broadcast_in_dim.78
  162.1 5.4 %all-to-all-start.6 = ((bf16[8,72,1024]{2,1,0:T(8,128)(2,1)}), bf16[8,72,1024]{2,1,0:T(8,128)(2,1)S(1)}, u32[]{:S(2)}, u32[]{:S(2)}) async-start(bf16[8,72,1024]{2,1,0:T(8,128)(2,1)} %broadcast_in_dim.78), calls=%async_computation.6 | async-start | bytes 2359296 | tf_op jit(solution)/shard_map/all_to_all | solution.py:23
  167.5 0.7 convert_reduce_fusion.2
  168.2 2.9 %convolution_convert_fusion = bf16[1024,512]{1,0:T(8,128)(2,1)} fusion(bf16[512,1024]{1,0:T(8,128)(2,1)} %bitcast.30, bf16[512,640]{1,0:T(8,128)(2,1)S(1)} %all_gather.31), kind=kOutput, calls=%fused_computation.2 | convolution fusion | flops 537395200 | bytes 2621440 | tf_op jit(solution)/shard_map/dot_general | solution.py:18
  171.1 12.5 %all-to-all-done.6 = bf16[8,72,1024]{2,1,0:T(8,128)(2,1)S(1)} async-done(((bf16[8,72,1024]{2,1,0:T(8,128)(2,1)}), bf16[8,72,1024]{2,1,0:T(8,128)(2,1)S(1)}, u32[]{:S(2)}, u32[]{:S(2)}) %all-to-all-start.6) | async-done | bytes 1179680 | tf_op jit(solution)/shard_map/all_to_all | solution.py:23
  183.7 0.6 fusion.8
  184.3 0.6 slice_add_fusion
  184.9 0.1 slice.37
  185.0 0.7 fusion
  185.7 1.3 copy.12
  (20 shorter events, 0.2 us)
Async XLA Ops:
  0.6 83.2 %copy-start = (bf16[1024,512]{1,0:T(8,128)(2,1)S(1)}, bf16[1024,512]{1,0:T(8,128)(2,1)}, u32[]{:S(2)}) copy-start(bf16[1024,512]{1,0:T(8,128)(2,1)} %param.10) | copy-start | bytes 3145732
  0.6 38.4 %copy-start.7 = (bf16[512,1024]{1,0:T(8,128)(2,1)S(1)}, bf16[512,1024]{1,0:T(8,128)(2,1)}, u32[]{:S(2)}) copy-start(bf16[512,1024]{1,0:T(8,128)(2,1)} %param.8) | copy-start | bytes 3145732
  39.0 0.8 copy-start.2
  62.6 0.7 copy-start.4
  65.1 18.8 %all-to-all-start.2 = ((bf16[8,64,1024]{2,1,0:T(8,128)(2,1)}), bf16[8,64,1024]{2,1,0:T(8,128)(2,1)S(1)}, u32[]{:S(2)}, u32[]{:S(2)}) async-start(bf16[8,64,1024]{2,1,0:T(8,128)(2,1)} %broadcast_in_dim.68), calls=%async_computation.2 | async-start | bytes 2097152 | tf_op jit(solution)/shard_map/all_to_all | solution.py:23
  83.8 10.0 %copy-start.1 = (bf16[8,64,1024]{2,1,0:T(8,128)(2,1)}, bf16[8,64,1024]{2,1,0:T(8,128)(2,1)S(1)}, u32[]{:S(2)}) copy-start(bf16[8,64,1024]{2,1,0:T(8,128)(2,1)S(1)} %all-to-all-done.2) | copy-start | bytes 3145732
  86.8 25.0 %copy-start.5 = (bf16[8,512]{1,0:T(8,128)(2,1)S(1)}, bf16[8,512]{1,0:T(8,128)(2,1)}, u32[]{:S(2)}) copy-start(bf16[8,512]{1,0:T(8,128)(2,1)} %param.7) | copy-start | bytes 24580
  86.8 25.0 %copy-start.6 = (f32[512]{0:T(512)S(1)}, f32[512]{0:T(512)}, u32[]{:S(2)}) copy-start(f32[512]{0:T(512)} %param.11) | copy-start | bytes 6148
  93.8 18.0 %all-to-all-start.3 = ((bf16[16,8,512]{2,1,0:T(8,128)(2,1)}), bf16[16,8,512]{2,1,0:T(8,128)(2,1)S(1)}, u32[]{:S(2)}, u32[]{:S(2)}) async-start(bf16[16,8,512]{2,1,0:T(8,128)(2,1)} %fusion.4), calls=%async_computation.3 | async-start | bytes 262144 | tf_op jit(solution)/shard_map/all_to_all | solution.py:44
  140.3 20.2 %all-to-all-start.5 = ((bf16[8,64,1024]{2,1,0:T(8,128)(2,1)}), bf16[8,64,1024]{2,1,0:T(8,128)(2,1)S(1)}, u32[]{:S(2)}, u32[]{:S(2)}) async-start(bf16[8,64,1024]{2,1,0:T(8,128)(2,1)} %bitcast.31), calls=%async_computation.5 | async-start | bytes 2097152 | tf_op jit(solution)/shard_map/all_to_all | solution.py:49
  162.1 21.5 %all-to-all-start.6 = ((bf16[8,72,1024]{2,1,0:T(8,128)(2,1)}), bf16[8,72,1024]{2,1,0:T(8,128)(2,1)S(1)}, u32[]{:S(2)}, u32[]{:S(2)}) async-start(bf16[8,72,1024]{2,1,0:T(8,128)(2,1)} %broadcast_in_dim.78), calls=%async_computation.6 | async-start | bytes 2359296 | tf_op jit(solution)/shard_map/all_to_all | solution.py:23
  183.6 1.3 copy-start.3

commit v2 on v1

v2 whole, which is shorter than its diff:
```python
import math

import jax
import jax.numpy as jnp
from jax import lax
from jax.sharding import Mesh, PartitionSpec as P

sparsity = 0.03

SIZES = (4, 4, 2, 2, 2, 4)
ZH, ZL, XL, C, XH, Y = SIZES
LAT = ("zh", "zl", "xl", "c")
TOK = ("xh", "y")
N_TOK = XH * Y
bf16, f32 = jnp.bfloat16, jnp.float32
SWAP = [(0, 1), (1, 0)]


def dot(a, b, da, db):
    return lax.dot_general(a, b, (((da,), (db,)), ((), ())), preferred_element_type=f32)


def exchange(x, axes, n):
    parts = lax.all_to_all(x, axes, 0, 0, tiled=True)
    return parts.reshape(n, x.shape[0] // n, x.shape[1])


def share(x, axes, n):
    copies = jnp.broadcast_to(x[None], (n,) + x.shape).reshape(n * x.shape[0], x.shape[1])
    return exchange(copies, axes, n)


def pick(pair, which):
    return lax.dynamic_index_in_dim(pair, which, 0, keepdims=False)


def partner(x):
    return lax.ppermute(x, "xh", SWAP)


def together(*values):
    return lax.optimization_barrier(values)


def split2(v):
    high = v.astype(bf16)
    return high, (v - high.astype(f32)).astype(bf16)


def fold(x):
    x = jnp.sum(x.reshape(-1, 8, x.shape[1]), axis=0)
    return sum(x[:, i : i + 128] for i in range(0, x.shape[1], 128))


def with_lanes(x, tile):
    high, low = split2(tile)
    rest = jnp.zeros((x.shape[0] - 16, 128), bf16)
    return jnp.concatenate([x.astype(bf16), jnp.concatenate([high, low, rest], axis=0)], axis=1)


def local(inputs, targets, enc_weight, enc_bias, dec_weight, dec_bias):
    rows, width = inputs.shape
    lats = enc_weight.shape[1]
    total_rows = rows * ZH * ZL * XL * C
    full_width = width * N_TOK
    scale_root = math.sqrt(total_rows)
    xh, c, zh = lax.axis_index("xh"), lax.axis_index("c"), lax.axis_index("zh")

    dec_other = partner(dec_weight)
    x = share(inputs, ("zl", "zh"), ZL * ZH).reshape(-1, width)
    x = lax.all_gather(x, "xl", axis=0, tiled=True)
    x, dec_other = together(x, dec_other)
    every_row = lax.all_gather(x, "c", axis=0, tiled=True)
    pre = dot(every_row, enc_weight, 1, 0).astype(bf16)
    pre_parts = exchange(pre, TOK, N_TOK)
    my_target = lax.ppermute(
        targets.astype(f32) - dec_bias, ("c", "xh"), [(0, 0), (1, 2), (2, 1), (3, 3)]
    )
    pre_parts, my_target = together(pre_parts, my_target)
    preact = jnp.sum(pre_parts.astype(f32), axis=0) + enc_bias
    lifted = jnp.maximum(preact, 0.0)
    latent = lifted * lifted
    latent_sum = fold(latent)
    latent_low = lax.all_gather(latent.astype(bf16), "y", axis=0, tiled=True)

    same = c == xh
    recon_mine = dot(latent_low, dec_weight, 1, 0)
    recon_other = dot(latent_low, dec_other, 1, 0)
    send = jnp.where(same, recon_other, recon_mine).astype(bf16)
    both = lax.all_gather(send, "c", axis=0, tiled=False)
    part = jnp.where(same, recon_mine, recon_other) + pick(both, 1 - c).astype(f32)
    part = jnp.sum(exchange(part.astype(bf16), ("xl", "zl"), XL * ZL).astype(f32), axis=0)
    block = lax.broadcasted_iota(jnp.int32, (ZH, rows, width), 0)
    minus = jnp.where(block == zh, my_target[None], 0.0).reshape(ZH * rows, width)
    every = share(with_lanes(part - minus, latent_sum), "zh", ZH)
    every, lat_other = together(every, partner(latent_low))
    every = jnp.sum(every.astype(f32), axis=0)
    residual = every[:, :width]
    piece = 0.5 * fold(residual * residual) + sparsity * fold(every[:, width:])
    grad = with_lanes(residual / scale_root, piece)
    grad = share(grad, ("xl", "zl"), XL * ZL).reshape(-1, width + 128)
    grad = lax.all_gather(grad, "c", axis=0, tiled=False)
    lat_loss = jnp.sum(grad[:, :, width:].astype(f32))
    grad_mine = pick(grad, xh)[:, :width]
    grad_send = pick(grad, 1 - xh)[:, :width]

    back = (dot(grad_mine, dec_weight, 1, 1) + dot(grad_send, dec_other, 1, 1)).astype(bf16)
    back_parts, grad_recv = together(exchange(back, "y", Y), partner(grad_send))
    back_grad = jnp.sum(back_parts.astype(f32), axis=0) + sparsity / scale_root
    grad_dec_bias = jnp.sum(grad_mine.astype(f32), axis=0) + jnp.sum(
        grad_recv.astype(f32), axis=0
    )
    grad_dec = (dot(latent_low, grad_mine, 0, 0) + dot(lat_other, grad_recv, 0, 0)).astype(bf16)
    grad_pre = back_grad * (2.0 * lifted)

    high, low = split2(lat_loss)
    bias_high, bias_low = split2(jnp.sum(grad_pre, axis=0, keepdims=True))
    row = lax.broadcasted_iota(jnp.int32, (8, lats), 0)
    zero = jnp.zeros((8, lats), bf16)
    tail = jnp.where(row == 0, bias_high, jnp.where(row == 1, bias_low, zero))
    tail = jnp.where(row == 2, high, jnp.where(row == 3, low, tail))
    shared = share(jnp.concatenate([grad_pre.astype(bf16), tail], axis=0), TOK, N_TOK)
    slab = shared.shape[1] - 8
    grad_pre_low = shared[:, :slab].reshape(-1, lats)
    tails = jnp.sum(shared[:, slab:].astype(f32), axis=0)
    grad_enc_bias = tails[0] + tails[1]
    loss = (tails[2, 0] + tails[3, 0]) / (total_rows * full_width)
    grad_enc = dot(every_row, grad_pre_low, 0, 0).astype(bf16)
    return (loss, grad_enc, grad_dec, grad_enc_bias, grad_dec_bias)


def solution(mesh):
    fine = Mesh(mesh.devices.reshape(SIZES), LAT + TOK)
    in_specs = (
        P(LAT, TOK),
        P(LAT, TOK),
        P(TOK, LAT),
        P(LAT),
        P(LAT, TOK),
        P(TOK),
    )
    out_specs = (P(), P(TOK, LAT), P(LAT, TOK), P(LAT), P(TOK))
    return jax.shard_map(local, mesh=fine, in_specs=in_specs, out_specs=out_specs, check_vma=False)
```

time: 190 us -> 186 us (0.979)
  blocking collectives: 95.3 us -> 54.8 us
  starting transfers between devices: 19.8 us -> 41.5 us
  waiting for transfers between devices: 52.4 us -> 62.1 us
  matrix products: 6.81 us -> 12.6 us
    all_to_all x3 -> x1, blocking collectives: 70.8 us -> 29.1 us  [exchange(): parts = lax.all_to_all(x, axes, 0, 0, tiled=True)]
    ppermute x0 -> x4, starting transfers between devices: none -> 12 us  [the longest x3 11.3 us: partner(): return lax.ppermute(x, 'xh', SWAP)]
    all_to_all x4 -> x6, starting transfers between devices: 19.8 us -> 29.6 us  [exchange(): parts = lax.all_to_all(x, axes, 0, 0, tiled=True)]
    ppermute x0 -> x4, waiting for transfers between devices: none -> 7.02 us  [the longest x3 7.02 us: partner(): return lax.ppermute(x, 'xh', SWAP)]
    dot_general x5 -> x8, matrix products: 6.81 us -> 12.6 us  [dot(): lax.dot_general(a, b, (((da,), (db,)), ((), ())), preferred_element_type=...]
    all_to_all x4 -> x6, waiting for transfers between devices: 52.4 us -> 55.1 us  [exchange(): parts = lax.all_to_all(x, axes, 0, 0, tiled=True)]
    all_gather x6 -> x5, blocking collectives: 24.4 us -> 25.7 us  [the longest x1 13.4 us: local(): latent_low = lax.all_gather(latent.astype(bf16), 'y', axis=0, tiled=True)]
  transfers between devices with their start and end apart: 4 -> 10, of which waited for: 4 -> 7; matrix products, arithmetic and copies ran while one was open for 2% -> 4% of each run, Pallas kernels for 0% -> 0%
where the time goes in v2:
time: 186 us; the launch traced here: 185 us
  waiting for transfers between devices  62.1 us (33%)
  blocking collectives  54.8 us (29%)
  starting transfers between devices  41.5 us (22%)
  matrix products  12.6 us (7%)
  local copies, waits for them, and re-layouts  4.96 us (3%)
  between operations  4.68 us (3%)
  other arithmetic  4.46 us (2%)
    all_to_all x6, waiting for transfers between devices, exchange(): parts = lax.all_to_all(x, axes, 0, 0, tiled=True)  55.1 us
    all_to_all x6, starting transfers between devices, exchange(): parts = lax.all_to_all(x, axes, 0, 0, tiled=True)  29.6 us
    all_to_all x1, blocking collectives, exchange(): parts = lax.all_to_all(x, axes, 0, 0, tiled=True)  29.1 us
    all_gather x1, blocking collectives, local(): latent_low = lax.all_gather(latent.astype(bf16), 'y', axis=0, tiled=True)  13.4 us
    dot_general x8, matrix products, dot(): lax.dot_general(a, b, (((da,), (db,)), ((), ())), preferred_element_type=...  12.6 us
    ppermute x3, starting transfers between devices, partner(): return lax.ppermute(x, 'xh', SWAP)  11.3 us
    ppermute x3, waiting for transfers between devices, partner(): return lax.ppermute(x, 'xh', SWAP)  7.02 us
    all_gather x1, blocking collectives, local(): x = lax.all_gather(x, 'xl', axis=0, tiled=True)  5.63 us
  transfers between devices with their start and end apart: 10, of which 7 were waited for; matrix products, arithmetic and copies ran while one was open for 4% of the time, Pallas kernels for 0%

profile of v2, /device:TPU:8, one launch (start us, length us, event | category | flops | bytes accessed | tf_op | source)
XLA Modules:
  0.0 185.1 jit_solution(16853098364386196467)
XLA Ops:
  0.6 5.1 %collective-permute-start = (bf16[1024,512]{1,0:T(8,128)(2,1)}, bf16[1024,512]{1,0:T(8,128)(2,1)}, u32[]{:S(2)}, u32[]{:S(2)}) collective-permute-start(bf16[1024,512]{1,0:T(8,128)(2,1)} %param.10), channel_id=1, source_target_pairs={{0,4},{4,0},{1,5},{5,1},{2,6},{6,2},{3,7},{7,3},{8,12},{12,8},{9,1... | collective-permute-start | bytes 3145736 | tf_op jit(solution)/shard_map/ppermute | solution.py:38
  5.7 0.7 broadcast_in_dim.65
  6.4 29.1 %all_to_all.54 = bf16[16,8,512]{2,1,0:T(8,128)(2,1)S(1)} all-to-all(bf16[16,8,512]{2,1,0:T(8,128)(2,1)S(1)} %broadcast_in_dim.65), channel_id=1, replica_groups=mesh['zh'=4,'zl'=4,'xl'=2,'c'=2,'xh'=2,'y'=4] {'zl','zh'}, dimensions={0} | all-to-all | bytes 262144 | tf_op jit(solution)/shard_map/all_to_all | solution.py:24
  35.5 5.6 %all_gather.18 = bf16[256,512]{1,0:T(8,128)(2,1)S(1)} all-gather(bf16[128,512]{1,0:T(8,128)(2,1)S(1)} %bitcast.53), channel_id=1, replica_groups=mesh['zh'=4,'zl'=4,'xl'=2,'c'=2,'xh'=2,'y'=4] {'xl'}, dimensions={0}, use_global_device_ids=true | all-gather | bytes 393216 | tf_op jit(solution)/shard_map/all_gather | solution.py:71
  41.2 2.2 %all_gather.19 = bf16[512,512]{1,0:T(8,128)(2,1)S(1)} all-gather(bf16[256,512]{1,0:T(8,128)(2,1)S(1)} %all_gather.18), channel_id=1, replica_groups=mesh['zh'=4,'zl'=4,'xl'=2,'c'=2,'xh'=2,'y'=4] {'c'}, dimensions={0}, use_global_device_ids=true | all-gather | bytes 786432 | tf_op jit(solution)/shard_map/all_gather | solution.py:73
  43.3 1.7 convolution_convert_fusion.1
  45.0 5.0 %all-to-all-start.1 = ((bf16[8,64,1024]{2,1,0:T(8,128)(2,1)}), bf16[8,64,1024]{2,1,0:T(8,128)(2,1)S(1)}, u32[]{:S(2)}, u32[]{:S(2)}) async-start(bf16[8,64,1024]{2,1,0:T(8,128)(2,1)} %bitcast.51), calls=%async_computation.1 | async-start | bytes 2097152 | tf_op jit(solution)/shard_map/all_to_all | solution.py:24
  50.1 0.7 collective-permute-start.1
  50.8 14.2 %all-to-all-done.1 = bf16[8,64,1024]{2,1,0:T(8,128)(2,1)S(1)} async-done(((bf16[8,64,1024]{2,1,0:T(8,128)(2,1)}), bf16[8,64,1024]{2,1,0:T(8,128)(2,1)S(1)}, u32[]{:S(2)}, u32[]{:S(2)}) %all-to-all-start.1) | async-done | bytes 1048608 | tf_op jit(solution)/shard_map/all_to_all | solution.py:24
  65.0 0.2 convert_reduce_fusion
  65.2 13.4 %all_gather.20 = bf16[256,1024]{1,0:T(8,128)(2,1)S(1)} all-gather(bf16[64,1024]{1,0:T(8,128)(2,1)S(1)} %multiply_convert_fusion), channel_id=1, replica_groups=mesh['zh'=4,'zl'=4,'xl'=2,'c'=2,'xh'=2,'y'=4] {'y'}, dimensions={0}, use_global_device_ids=true | all-gather | bytes 655360 | tf_op jit(solution)/shard_map/all_gather | solution.py:84
  78.6 1.7 fusion.20
  80.3 1.7 select_convert_fusion
  82.0 2.2 %all-gather = bf16[512,512]{1,0:T(8,128)(2,1)S(1)} all-gather(bf16[256,512]{1,0:T(8,128)(2,1)S(1)} %get-tuple-element.33), channel_id=2, replica_groups=mesh['zh'=4,'zl'=4,'xl'=2,'c'=2,'xh'=2,'y'=4] {'c'}, dimensions={0}, use_global_device_ids=true | all-gather | bytes 786432 | tf_op jit(solution)/shard_map/all_gather | solution.py:90
  84.1 0.8 fusion.1
  85.0 4.7 %all-to-all-start.2 = ((bf16[8,32,512]{2,1,0:T(8,128)(2,1)}), bf16[8,32,512]{2,1,0:T(8,128)(2,1)S(1)}, u32[]{:S(2)}, u32[]{:S(2)}) async-start(bf16[8,32,512]{2,1,0:T(8,128)(2,1)} %bitcast.4), calls=%async_computation.2 | async-start | bytes 524288 | tf_op jit(solution)/shard_map/all_to_all | solution.py:24
  89.7 0.1 iota.30
  89.8 3.7 %collective-permute-start.2 = (bf16[256,1024]{1,0:T(8,128)(2,1)S(1)}, bf16[256,1024]{1,0:T(8,128)(2,1)}, u32[]{:S(2)}, u32[]{:S(2)}) collective-permute-start(bf16[256,1024]{1,0:T(8,128)(2,1)S(1)} %all_gather.20), channel_id=1, source_target_pairs={{0,4},{4,0},{1,5},{5,1},{2,6},{6,2},{3,7},{7,3},{8,12},{12,8},{9,1... | collective-permute-start | bytes 1572872 | tf_op jit(solution)/shard_map/ppermute | solution.py:38
  93.6 6.1 %all-to-all-done.2 = bf16[8,32,512]{2,1,0:T(8,128)(2,1)S(1)} async-done(((bf16[8,32,512]{2,1,0:T(8,128)(2,1)}), bf16[8,32,512]{2,1,0:T(8,128)(2,1)S(1)}, u32[]{:S(2)}, u32[]{:S(2)}) %all-to-all-start.2) | async-done | bytes 262176 | tf_op jit(solution)/shard_map/all_to_all | solution.py:24
  99.8 0.1 fusion.10
  99.9 0.7 broadcast_in_dim.69
  100.6 6.6 %all-to-all-start.3 = ((bf16[4,32,640]{2,1,0:T(8,128)(2,1)}), bf16[4,32,640]{2,1,0:T(8,128)(2,1)S(1)}, u32[]{:S(2)}, u32[]{:S(2)}) async-start(bf16[4,32,640]{2,1,0:T(8,128)(2,1)} %broadcast_in_dim.69), calls=%async_computation.3 | async-start | bytes 327680 | tf_op jit(solution)/shard_map/all_to_all | solution.py:24
  107.2 1.3 collective-permute-done.2
  108.5 13.5 %all-to-all-done.3 = bf16[4,32,640]{2,1,0:T(8,128)(2,1)S(1)} async-done(((bf16[4,32,640]{2,1,0:T(8,128)(2,1)}), bf16[4,32,640]{2,1,0:T(8,128)(2,1)S(1)}, u32[]{:S(2)}, u32[]{:S(2)}) %all-to-all-start.3) | async-done | bytes 163872 | tf_op jit(solution)/shard_map/all_to_all | solution.py:24
  122.1 0.8 broadcast_in_dim.70
  122.8 3.5 %all-to-all-start.4 = ((bf16[8,32,640]{2,1,0:T(8,128)(2,1)}), bf16[8,32,640]{2,1,0:T(8,128)(2,1)S(1)}, u32[]{:S(2)}, u32[]{:S(2)}) async-start(bf16[8,32,640]{2,1,0:T(8,128)(2,1)} %broadcast_in_dim.70), calls=%async_computation.4 | async-start | bytes 655360 | tf_op jit(solution)/shard_map/all_to_all | solution.py:24
  126.4 10.2 %all-to-all-done.4 = bf16[8,32,640]{2,1,0:T(8,128)(2,1)S(1)} async-done(((bf16[8,32,640]{2,1,0:T(8,128)(2,1)}), bf16[8,32,640]{2,1,0:T(8,128)(2,1)S(1)}, u32[]{:S(2)}, u32[]{:S(2)}) %all-to-all-start.4) | async-done | bytes 327712 | tf_op jit(solution)/shard_map/all_to_all | solution.py:24
  136.6 2.3 %all_gather.23 = bf16[2,256,640]{2,1,0:T(8,128)(2,1)S(1)} all-gather(bf16[1,256,640]{2,1,0:T(8,128)(2,1)S(1)} %bitcast.49), channel_id=1, replica_groups=mesh['zh'=4,'zl'=4,'xl'=2,'c'=2,'xh'=2,'y'=4] {'c'}, dimensions={0}, use_global_device_ids=true | all-gather | bytes 983040 | tf_op jit(solution)/shard_map/all_gather | solution.py:102
  138.9 0.5 fusion.7
  139.4 0.3 copy-done.2
  139.7 2.5 %fusion = bf16[256,1024]{1,0:T(8,128)(2,1)} fusion(f32[256,1024]{1,0:T(8,128)S(1)} %fusion.7, bf16[1024,512]{1,0:T(8,128)(2,1)} %collective-permute-done, bf16[256,640]{1,0:T(8,128)(2,1)S(1)} %get-tuple-element.27), kind=kOutput, calls=%fused_computation.5 | convolution fusion | flops 268959744 | bytes 2883584 | tf_op jit(solution)/shard_map/dot_general | solution.py:20
  142.2 4.5 %all-to-all-start.5 = ((bf16[4,64,1024]{2,1,0:T(8,128)(2,1)}), bf16[4,64,1024]{2,1,0:T(8,128)(2,1)S(1)}, u32[]{:S(2)}, u32[]{:S(2)}) async-start(bf16[4,64,1024]{2,1,0:T(8,128)(2,1)} %bitcast.12), calls=%async_computation.5 | async-start | bytes 1048576 | tf_op jit(solution)/shard_map/all_to_all | solution.py:24
  146.7 2.5 %collective-permute-start.3 = (bf16[256,512]{1,0:T(8,128)(2,1)S(1)}, bf16[256,512]{1,0:T(8,128)(2,1)S(1)}, u32[]{:S(2)}, u32[]{:S(2)}) collective-permute-start(bf16[256,512]{1,0:T(8,128)(2,1)S(1)} %slice.107), channel_id=1, source_target_pairs={{0,4},{4,0},{1,5},{5,1},{2,6},{6,2},{3,7},{7,3},{8,12},{12,8},{9,1... | collective-permute-start | bytes 786440 | tf_op jit(solution)/shard_map/ppermute | solution.py:38
  149.3 1.6 convert_reduce_fusion.7
  152.2 5.7 %collective-permute-done.3 = bf16[256,512]{1,0:T(8,128)(2,1)S(1)} collective-permute-done((bf16[256,512]{1,0:T(8,128)(2,1)S(1)}, bf16[256,512]{1,0:T(8,128)(2,1)S(1)}, u32[]{:S(2)}, u32[]{:S(2)}) %collective-permute-start.3) | collective-permute-done | bytes 262176 | tf_op jit(solution)/shard_map/ppermute | solution.py:38
  157.9 0.1 convert_reduce_fusion.1
  158.1 0.1 select_select_fusion
  158.2 1.2 broadcast_in_dim.76
  159.3 5.1 %all-to-all-start.6 = ((bf16[8,72,1024]{2,1,0:T(8,128)(2,1)}), bf16[8,72,1024]{2,1,0:T(8,128)(2,1)S(1)}, u32[]{:S(2)}, u32[]{:S(2)}) async-start(bf16[8,72,1024]{2,1,0:T(8,128)(2,1)} %broadcast_in_dim.76), calls=%async_computation.6 | async-start | bytes 2359296 | tf_op jit(solution)/shard_map/all_to_all | solution.py:24
  164.5 0.5 fusion.5
  165.0 0.4 copy-done.4
  165.5 0.6 add.113
  166.1 2.5 %add_convert_fusion = bf16[1024,512]{1,0:T(8,128)(2,1)} fusion(f32[1024,512]{1,0:T(8,128)S(1)} %fusion.5, bf16[256,1024]{1,0:T(8,128)(2,1)} %collective-permute-done.2, bf16[256,512]{1,0:T(8,128)(2,1)S(1)} %copy-done.4), kind=kOutput, calls=%fused_computation | convolution fusion | flops 269484032 | bytes 3932160 | tf_op jit(solution)/shard_map/dot_general | solution.py:20
  168.5 11.1 %all-to-all-done.6 = bf16[8,72,1024]{2,1,0:T(8,128)(2,1)S(1)} async-done(((bf16[8,72,1024]{2,1,0:T(8,128)(2,1)}), bf16[8,72,1024]{2,1,0:T(8,128)(2,1)S(1)}, u32[]{:S(2)}, u32[]{:S(2)}) %all-to-all-start.6) | async-done | bytes 1179680 | tf_op jit(solution)/shard_map/all_to_all | solution.py:24
  179.6 0.6 fusion.19
  180.2 0.6 slice_add_fusion
  180.8 0.1 slice.112
  180.9 1.7 convolution_convert_fusion
  (46 shorter events, 0.7 us)
Async XLA Ops:
  0.6 42.7 %copy-start = (bf16[512,1024]{1,0:T(8,128)(2,1)S(1)}, bf16[512,1024]{1,0:T(8,128)(2,1)}, u32[]{:S(2)}) copy-start(bf16[512,1024]{1,0:T(8,128)(2,1)} %param.8) | copy-start | bytes 3145732
  0.6 40.5 %collective-permute-start = (bf16[1024,512]{1,0:T(8,128)(2,1)}, bf16[1024,512]{1,0:T(8,128)(2,1)}, u32[]{:S(2)}, u32[]{:S(2)}) collective-permute-start(bf16[1024,512]{1,0:T(8,128)(2,1)} %param.10), channel_id=1, source_target_pairs={{0,4},{4,0},{1,5},{5,1},{2,6},{6,2},{3,7},{7,3},{8,12},{12,8},{9,1... | collective-permute-start | bytes 3145736 | tf_op jit(solution)/shard_map/ppermute | solution.py:38
  43.3 1.7 copy-start.5
  43.3 6.8 %copy-start.8 = (bf16[8,512]{1,0:T(8,128)(2,1)S(1)}, bf16[8,512]{1,0:T(8,128)(2,1)}, u32[]{:S(2)}) copy-start(bf16[8,512]{1,0:T(8,128)(2,1)} %param.7) | copy-start | bytes 24580
  43.3 6.8 %copy-start.9 = (f32[512]{0:T(512)S(1)}, f32[512]{0:T(512)}, u32[]{:S(2)}) copy-start(f32[512]{0:T(512)} %param.11) | copy-start | bytes 6148
  45.0 20.1 %copy-start.7 = (f32[1024]{0:T(1024)S(1)}, f32[1024]{0:T(1024)}, u32[]{:S(2)}) copy-start(f32[1024]{0:T(1024)} %param.9) | copy-start | bytes 12292
  45.0 19.9 %all-to-all-start.1 = ((bf16[8,64,1024]{2,1,0:T(8,128)(2,1)}), bf16[8,64,1024]{2,1,0:T(8,128)(2,1)S(1)}, u32[]{:S(2)}, u32[]{:S(2)}) async-start(bf16[8,64,1024]{2,1,0:T(8,128)(2,1)} %bitcast.51), calls=%async_computation.1 | async-start | bytes 2097152 | tf_op jit(solution)/shard_map/all_to_all | solution.py:24
  50.1 0.7 collective-permute-start.1
  85.0 14.8 %all-to-all-start.2 = ((bf16[8,32,512]{2,1,0:T(8,128)(2,1)}), bf16[8,32,512]{2,1,0:T(8,128)(2,1)S(1)}, u32[]{:S(2)}, u32[]{:S(2)}) async-start(bf16[8,32,512]{2,1,0:T(8,128)(2,1)} %bitcast.4), calls=%async_computation.2 | async-start | bytes 524288 | tf_op jit(solution)/shard_map/all_to_all | solution.py:24
  89.8 18.6 %collective-permute-start.2 = (bf16[256,1024]{1,0:T(8,128)(2,1)S(1)}, bf16[256,1024]{1,0:T(8,128)(2,1)}, u32[]{:S(2)}, u32[]{:S(2)}) collective-permute-start(bf16[256,1024]{1,0:T(8,128)(2,1)S(1)} %all_gather.20), channel_id=1, source_target_pairs={{0,4},{4,0},{1,5},{5,1},{2,6},{6,2},{3,7},{7,3},{8,12},{12,8},{9,1... | collective-permute-start | bytes 1572872 | tf_op jit(solution)/shard_map/ppermute | solution.py:38
  100.6 38.4 %copy-start.1 = (bf16[1024,512]{1,0:T(8,128)(2,1)S(1)}, bf16[1024,512]{1,0:T(8,128)(2,1)}, u32[]{:S(2)}) copy-start(bf16[1024,512]{1,0:T(8,128)(2,1)} %param.10) | copy-start | bytes 3145732
  100.6 21.4 %all-to-all-start.3 = ((bf16[4,32,640]{2,1,0:T(8,128)(2,1)}), bf16[4,32,640]{2,1,0:T(8,128)(2,1)S(1)}, u32[]{:S(2)}, u32[]{:S(2)}) async-start(bf16[4,32,640]{2,1,0:T(8,128)(2,1)} %broadcast_in_dim.69), calls=%async_computation.3 | async-start | bytes 327680 | tf_op jit(solution)/shard_map/all_to_all | solution.py:24
  122.8 13.8 %all-to-all-start.4 = ((bf16[8,32,640]{2,1,0:T(8,128)(2,1)}), bf16[8,32,640]{2,1,0:T(8,128)(2,1)S(1)}, u32[]{:S(2)}, u32[]{:S(2)}) async-start(bf16[8,32,640]{2,1,0:T(8,128)(2,1)} %broadcast_in_dim.70), calls=%async_computation.4 | async-start | bytes 655360 | tf_op jit(solution)/shard_map/all_to_all | solution.py:24
  138.9 0.8 copy-start.2
  142.2 15.7 %all-to-all-start.5 = ((bf16[4,64,1024]{2,1,0:T(8,128)(2,1)}), bf16[4,64,1024]{2,1,0:T(8,128)(2,1)S(1)}, u32[]{:S(2)}, u32[]{:S(2)}) async-start(bf16[4,64,1024]{2,1,0:T(8,128)(2,1)} %bitcast.12), calls=%async_computation.5 | async-start | bytes 1048576 | tf_op jit(solution)/shard_map/all_to_all | solution.py:24
  146.7 11.2 %collective-permute-start.3 = (bf16[256,512]{1,0:T(8,128)(2,1)S(1)}, bf16[256,512]{1,0:T(8,128)(2,1)S(1)}, u32[]{:S(2)}, u32[]{:S(2)}) collective-permute-start(bf16[256,512]{1,0:T(8,128)(2,1)S(1)} %slice.107), channel_id=1, source_target_pairs={{0,4},{4,0},{1,5},{5,1},{2,6},{6,2},{3,7},{7,3},{8,12},{12,8},{9,1... | collective-permute-start | bytes 786440 | tf_op jit(solution)/shard_map/ppermute | solution.py:38
  157.9 1.4 copy-start.3
  159.3 20.3 %all-to-all-start.6 = ((bf16[8,72,1024]{2,1,0:T(8,128)(2,1)}), bf16[8,72,1024]{2,1,0:T(8,128)(2,1)S(1)}, u32[]{:S(2)}, u32[]{:S(2)}) async-start(bf16[8,72,1024]{2,1,0:T(8,128)(2,1)} %broadcast_in_dim.76), calls=%async_computation.6 | async-start | bytes 2359296 | tf_op jit(solution)/shard_map/all_to_all | solution.py:24
  164.5 0.9 copy-start.4
  168.5 12.4 %copy-start.6 = (bf16[512,512]{1,0:T(8,128)(2,1)S(1)}, bf16[512,512]{1,0:T(8,128)(2,1)}, u32[]{:S(2)}) copy-start(bf16[512,512]{1,0:T(8,128)(2,1)} %copy-done.5) | copy-start | bytes 1572868

commit v3 on v2

--- a/solution.py
+++ b/solution.py
@@ -105,7 +105,9 @@
     grad_send = pick(grad, 1 - xh)[:, :width]
 
     back = (dot(grad_mine, dec_weight, 1, 1) + dot(grad_send, dec_other, 1, 1)).astype(bf16)
-    back_parts, grad_recv = together(exchange(back, "y", Y), partner(grad_send))
+    fetch = pick(grad_send.reshape(2, -1, width), lax.axis_index("c"))
+    back_parts, grad_recv = together(exchange(back, "y", Y), partner(fetch))
+    grad_recv = lax.all_gather(grad_recv, "c", axis=0, tiled=True)
     back_grad = jnp.sum(back_parts.astype(f32), axis=0) + sparsity / scale_root
     grad_dec_bias = jnp.sum(grad_mine.astype(f32), axis=0) + jnp.sum(
         grad_recv.astype(f32), axis=0

time: 186 us -> 183 us (0.984)
  waiting for transfers between devices: 62.1 us -> 57.7 us
  blocking collectives: 54.8 us -> 56.8 us
    ppermute x3, waiting for transfers between devices: 7.02 us -> 4.22 us  [partner(): return lax.ppermute(x, 'xh', SWAP)]
    all_gather x0 -> x1, blocking collectives: none -> 1.99 us  [local(): grad_recv = lax.all_gather(grad_recv, 'c', axis=0, tiled=True)]
where the time goes in v3:
time: 183 us; the launch traced here: 182 us
  waiting for transfers between devices  57.7 us (32%)
  blocking collectives  56.8 us (31%)
  starting transfers between devices  41.5 us (23%)
  matrix products  12.6 us (7%)
  between operations  4.68 us (3%)
  local copies, waits for them, and re-layouts  4.55 us (2%)
  other arithmetic  4.46 us (2%)
    all_to_all x6, waiting for transfers between devices, exchange(): parts = lax.all_to_all(x, axes, 0, 0, tiled=True)  53.5 us
    all_to_all x6, starting transfers between devices, exchange(): parts = lax.all_to_all(x, axes, 0, 0, tiled=True)  29.6 us
    all_to_all x1, blocking collectives, exchange(): parts = lax.all_to_all(x, axes, 0, 0, tiled=True)  29.1 us
    all_gather x1, blocking collectives, local(): latent_low = lax.all_gather(latent.astype(bf16), 'y', axis=0, tiled=True)  13.4 us
    dot_general x8, matrix products, dot(): lax.dot_general(a, b, (((da,), (db,)), ((), ())), preferred_element_type=...  12.6 us
    ppermute x3, starting transfers between devices, partner(): return lax.ppermute(x, 'xh', SWAP)  11.3 us
    all_gather x1, blocking collectives, local(): x = lax.all_gather(x, 'xl', axis=0, tiled=True)  5.63 us
    ppermute x3, waiting for transfers between devices, partner(): return lax.ppermute(x, 'xh', SWAP)  4.22 us
  transfers between devices with their start and end apart: 10, of which 7 were waited for; matrix products, arithmetic and copies ran while one was open for 4% of the time, Pallas kernels for 0%

profile of v3, /device:TPU:8, one launch (start us, length us, event | category | flops | bytes accessed | tf_op | source)
XLA Modules:
  0.0 182.3 jit_solution(7101769398528998860)
XLA Ops:
  0.6 5.1 %collective-permute-start = (bf16[1024,512]{1,0:T(8,128)(2,1)}, bf16[1024,512]{1,0:T(8,128)(2,1)}, u32[]{:S(2)}, u32[]{:S(2)}) collective-permute-start(bf16[1024,512]{1,0:T(8,128)(2,1)} %param.10), channel_id=1, source_target_pairs={{0,4},{4,0},{1,5},{5,1},{2,6},{6,2},{3,7},{7,3},{8,12},{12,8},{9,1... | collective-permute-start | bytes 3145736 | tf_op jit(solution)/shard_map/ppermute | solution.py:38
  5.7 0.7 broadcast_in_dim.65
  6.4 29.1 %all_to_all.54 = bf16[16,8,512]{2,1,0:T(8,128)(2,1)S(1)} all-to-all(bf16[16,8,512]{2,1,0:T(8,128)(2,1)S(1)} %broadcast_in_dim.65), channel_id=1, replica_groups=mesh['zh'=4,'zl'=4,'xl'=2,'c'=2,'xh'=2,'y'=4] {'zl','zh'}, dimensions={0} | all-to-all | bytes 262144 | tf_op jit(solution)/shard_map/all_to_all | solution.py:24
  35.5 5.6 %all_gather.21 = bf16[256,512]{1,0:T(8,128)(2,1)S(1)} all-gather(bf16[128,512]{1,0:T(8,128)(2,1)S(1)} %bitcast.57), channel_id=1, replica_groups=mesh['zh'=4,'zl'=4,'xl'=2,'c'=2,'xh'=2,'y'=4] {'xl'}, dimensions={0}, use_global_device_ids=true | all-gather | bytes 393216 | tf_op jit(solution)/shard_map/all_gather | solution.py:71
  41.2 2.2 %all_gather.22 = bf16[512,512]{1,0:T(8,128)(2,1)S(1)} all-gather(bf16[256,512]{1,0:T(8,128)(2,1)S(1)} %all_gather.21), channel_id=1, replica_groups=mesh['zh'=4,'zl'=4,'xl'=2,'c'=2,'xh'=2,'y'=4] {'c'}, dimensions={0}, use_global_device_ids=true | all-gather | bytes 786432 | tf_op jit(solution)/shard_map/all_gather | solution.py:73
  43.3 1.7 convolution_convert_fusion.1
  45.0 5.0 %all-to-all-start.1 = ((bf16[8,64,1024]{2,1,0:T(8,128)(2,1)}), bf16[8,64,1024]{2,1,0:T(8,128)(2,1)S(1)}, u32[]{:S(2)}, u32[]{:S(2)}) async-start(bf16[8,64,1024]{2,1,0:T(8,128)(2,1)} %bitcast.54), calls=%async_computation.1 | async-start | bytes 2097152 | tf_op jit(solution)/shard_map/all_to_all | solution.py:24
  50.1 0.7 collective-permute-start.1
  50.8 14.2 %all-to-all-done.1 = bf16[8,64,1024]{2,1,0:T(8,128)(2,1)S(1)} async-done(((bf16[8,64,1024]{2,1,0:T(8,128)(2,1)}), bf16[8,64,1024]{2,1,0:T(8,128)(2,1)S(1)}, u32[]{:S(2)}, u32[]{:S(2)}) %all-to-all-start.1) | async-done | bytes 1048608 | tf_op jit(solution)/shard_map/all_to_all | solution.py:24
  65.0 0.2 convert_reduce_fusion
  65.2 13.4 %all_gather.23 = bf16[256,1024]{1,0:T(8,128)(2,1)S(1)} all-gather(bf16[64,1024]{1,0:T(8,128)(2,1)S(1)} %multiply_convert_fusion), channel_id=1, replica_groups=mesh['zh'=4,'zl'=4,'xl'=2,'c'=2,'xh'=2,'y'=4] {'y'}, dimensions={0}, use_global_device_ids=true | all-gather | bytes 655360 | tf_op jit(solution)/shard_map/all_gather | solution.py:84
  78.6 1.7 fusion.20
  80.3 1.7 select_convert_fusion
  82.0 2.2 %all-gather = bf16[512,512]{1,0:T(8,128)(2,1)S(1)} all-gather(bf16[256,512]{1,0:T(8,128)(2,1)S(1)} %get-tuple-element.33), channel_id=2, replica_groups=mesh['zh'=4,'zl'=4,'xl'=2,'c'=2,'xh'=2,'y'=4] {'c'}, dimensions={0}, use_global_device_ids=true | all-gather | bytes 786432 | tf_op jit(solution)/shard_map/all_gather | solution.py:90
  84.1 0.8 fusion.1
  85.0 4.7 %all-to-all-start.2 = ((bf16[8,32,512]{2,1,0:T(8,128)(2,1)}), bf16[8,32,512]{2,1,0:T(8,128)(2,1)S(1)}, u32[]{:S(2)}, u32[]{:S(2)}) async-start(bf16[8,32,512]{2,1,0:T(8,128)(2,1)} %bitcast.4), calls=%async_computation.2 | async-start | bytes 524288 | tf_op jit(solution)/shard_map/all_to_all | solution.py:24
  89.7 0.1 iota.30
  89.8 3.7 %collective-permute-start.2 = (bf16[256,1024]{1,0:T(8,128)(2,1)S(1)}, bf16[256,1024]{1,0:T(8,128)(2,1)}, u32[]{:S(2)}, u32[]{:S(2)}) collective-permute-start(bf16[256,1024]{1,0:T(8,128)(2,1)S(1)} %all_gather.23), channel_id=1, source_target_pairs={{0,4},{4,0},{1,5},{5,1},{2,6},{6,2},{3,7},{7,3},{8,12},{12,8},{9,1... | collective-permute-start | bytes 1572872 | tf_op jit(solution)/shard_map/ppermute | solution.py:38
  93.6 6.1 %all-to-all-done.2 = bf16[8,32,512]{2,1,0:T(8,128)(2,1)S(1)} async-done(((bf16[8,32,512]{2,1,0:T(8,128)(2,1)}), bf16[8,32,512]{2,1,0:T(8,128)(2,1)S(1)}, u32[]{:S(2)}, u32[]{:S(2)}) %all-to-all-start.2) | async-done | bytes 262176 | tf_op jit(solution)/shard_map/all_to_all | solution.py:24
  99.8 0.1 fusion.10
  99.9 0.7 broadcast_in_dim.69
  100.6 6.6 %all-to-all-start.3 = ((bf16[4,32,640]{2,1,0:T(8,128)(2,1)}), bf16[4,32,640]{2,1,0:T(8,128)(2,1)S(1)}, u32[]{:S(2)}, u32[]{:S(2)}) async-start(bf16[4,32,640]{2,1,0:T(8,128)(2,1)} %broadcast_in_dim.69), calls=%async_computation.3 | async-start | bytes 327680 | tf_op jit(solution)/shard_map/all_to_all | solution.py:24
  107.2 1.3 collective-permute-done.2
  108.5 13.5 %all-to-all-done.3 = bf16[4,32,640]{2,1,0:T(8,128)(2,1)S(1)} async-done(((bf16[4,32,640]{2,1,0:T(8,128)(2,1)}), bf16[4,32,640]{2,1,0:T(8,128)(2,1)S(1)}, u32[]{:S(2)}, u32[]{:S(2)}) %all-to-all-start.3) | async-done | bytes 163872 | tf_op jit(solution)/shard_map/all_to_all | solution.py:24
  122.1 0.8 broadcast_in_dim.70
  122.8 3.5 %all-to-all-start.4 = ((bf16[8,32,640]{2,1,0:T(8,128)(2,1)}), bf16[8,32,640]{2,1,0:T(8,128)(2,1)S(1)}, u32[]{:S(2)}, u32[]{:S(2)}) async-start(bf16[8,32,640]{2,1,0:T(8,128)(2,1)} %broadcast_in_dim.70), calls=%async_computation.4 | async-start | bytes 655360 | tf_op jit(solution)/shard_map/all_to_all | solution.py:24
  126.4 10.2 %all-to-all-done.4 = bf16[8,32,640]{2,1,0:T(8,128)(2,1)S(1)} async-done(((bf16[8,32,640]{2,1,0:T(8,128)(2,1)}), bf16[8,32,640]{2,1,0:T(8,128)(2,1)S(1)}, u32[]{:S(2)}, u32[]{:S(2)}) %all-to-all-start.4) | async-done | bytes 327712 | tf_op jit(solution)/shard_map/all_to_all | solution.py:24
  136.6 2.3 %all_gather.26 = bf16[2,256,640]{2,1,0:T(8,128)(2,1)S(1)} all-gather(bf16[1,256,640]{2,1,0:T(8,128)(2,1)S(1)} %bitcast.52), channel_id=1, replica_groups=mesh['zh'=4,'zl'=4,'xl'=2,'c'=2,'xh'=2,'y'=4] {'c'}, dimensions={0}, use_global_device_ids=true | all-gather | bytes 983040 | tf_op jit(solution)/shard_map/all_gather | solution.py:102
  138.9 0.5 fusion.7
  139.4 0.3 copy-done.2
  139.7 2.5 %fusion = bf16[256,1024]{1,0:T(8,128)(2,1)} fusion(f32[256,1024]{1,0:T(8,128)S(1)} %fusion.7, bf16[1024,512]{1,0:T(8,128)(2,1)} %collective-permute-done, bf16[256,640]{1,0:T(8,128)(2,1)S(1)} %get-tuple-element.27), kind=kOutput, calls=%fused_computation.5 | convolution fusion | flops 268959744 | bytes 2883584 | tf_op jit(solution)/shard_map/dot_general | solution.py:20
  142.2 4.5 %all-to-all-start.5 = ((bf16[4,64,1024]{2,1,0:T(8,128)(2,1)}), bf16[4,64,1024]{2,1,0:T(8,128)(2,1)S(1)}, u32[]{:S(2)}, u32[]{:S(2)}) async-start(bf16[4,64,1024]{2,1,0:T(8,128)(2,1)} %bitcast.12), calls=%async_computation.5 | async-start | bytes 1048576 | tf_op jit(solution)/shard_map/all_to_all | solution.py:24
  146.7 2.5 %collective-permute-start.3 = (bf16[128,512]{1,0:T(8,128)(2,1)S(1)}, bf16[128,512]{1,0:T(8,128)(2,1)S(1)}, u32[]{:S(2)}, u32[]{:S(2)}) collective-permute-start(bf16[128,512]{1,0:T(8,128)(2,1)S(1)} %dynamic-slice_bitcast_fusion.2), channel_id=1, source_target_pairs={{0,4},{4,0},{1,5},{5,1},{2,6},{6,2},{3,7},{7,3},{8,12},{12,8},{9,1... | collective-permute-start | bytes 393224 | tf_op jit(solution)/shard_map/ppermute | solution.py:38
  149.3 1.6 convert_reduce_fusion.7
  152.2 2.9 %collective-permute-done.3 = bf16[128,512]{1,0:T(8,128)(2,1)S(1)} collective-permute-done((bf16[128,512]{1,0:T(8,128)(2,1)S(1)}, bf16[128,512]{1,0:T(8,128)(2,1)S(1)}, u32[]{:S(2)}, u32[]{:S(2)}) %collective-permute-start.3) | collective-permute-done | bytes 131104 | tf_op jit(solution)/shard_map/ppermute | solution.py:38
  155.1 0.1 convert_reduce_fusion.1
  155.3 0.1 select_select_fusion
  155.4 1.2 broadcast_in_dim.76
  156.5 5.1 %all-to-all-start.6 = ((bf16[8,72,1024]{2,1,0:T(8,128)(2,1)}), bf16[8,72,1024]{2,1,0:T(8,128)(2,1)S(1)}, u32[]{:S(2)}, u32[]{:S(2)}) async-start(bf16[8,72,1024]{2,1,0:T(8,128)(2,1)} %broadcast_in_dim.76), calls=%async_computation.6 | async-start | bytes 2359296 | tf_op jit(solution)/shard_map/all_to_all | solution.py:24
  161.7 0.5 fusion.5
  162.2 2.0 %all_gather.27 = bf16[256,512]{1,0:T(8,128)(2,1)S(1)} all-gather(bf16[128,512]{1,0:T(8,128)(2,1)S(1)} %collective-permute-done.3), channel_id=1, replica_groups=mesh['zh'=4,'zl'=4,'xl'=2,'c'=2,'xh'=2,'y'=4] {'c'}, dimensions={0}, use_global_device_ids=true | all-gather | bytes 393216 | tf_op jit(solution)/shard_map/all_gather | solution.py:110
  164.3 0.6 add.118
  164.8 2.5 %add_convert_fusion = bf16[1024,512]{1,0:T(8,128)(2,1)} fusion(f32[1024,512]{1,0:T(8,128)S(1)} %fusion.5, bf16[256,1024]{1,0:T(8,128)(2,1)} %collective-permute-done.2, bf16[256,512]{1,0:T(8,128)(2,1)S(1)} %all_gather.27), kind=kOutput, calls=%fused_computation | convolution fusion | flops 269484032 | bytes 3932160 | tf_op jit(solution)/shard_map/dot_general | solution.py:20
  167.3 9.5 %all-to-all-done.6 = bf16[8,72,1024]{2,1,0:T(8,128)(2,1)S(1)} async-done(((bf16[8,72,1024]{2,1,0:T(8,128)(2,1)}), bf16[8,72,1024]{2,1,0:T(8,128)(2,1)S(1)}, u32[]{:S(2)}, u32[]{:S(2)}) %all-to-all-start.6) | async-done | bytes 1179680 | tf_op jit(solution)/shard_map/all_to_all | solution.py:24
  176.8 0.6 fusion.19
  177.4 0.6 slice_add_fusion
  178.0 0.1 slice.112
  178.1 1.7 convolution_convert_fusion
  (44 shorter events, 0.7 us)
Async XLA Ops:
  0.6 42.7 %copy-start = (bf16[512,1024]{1,0:T(8,128)(2,1)S(1)}, bf16[512,1024]{1,0:T(8,128)(2,1)}, u32[]{:S(2)}) copy-start(bf16[512,1024]{1,0:T(8,128)(2,1)} %param.8) | copy-start | bytes 3145732
  0.6 40.5 %collective-permute-start = (bf16[1024,512]{1,0:T(8,128)(2,1)}, bf16[1024,512]{1,0:T(8,128)(2,1)}, u32[]{:S(2)}, u32[]{:S(2)}) collective-permute-start(bf16[1024,512]{1,0:T(8,128)(2,1)} %param.10), channel_id=1, source_target_pairs={{0,4},{4,0},{1,5},{5,1},{2,6},{6,2},{3,7},{7,3},{8,12},{12,8},{9,1... | collective-permute-start | bytes 3145736 | tf_op jit(solution)/shard_map/ppermute | solution.py:38
  43.3 1.7 copy-start.3
  43.3 6.8 %copy-start.6 = (bf16[8,512]{1,0:T(8,128)(2,1)S(1)}, bf16[8,512]{1,0:T(8,128)(2,1)}, u32[]{:S(2)}) copy-start(bf16[8,512]{1,0:T(8,128)(2,1)} %param.7) | copy-start | bytes 24580
  43.3 6.8 %copy-start.7 = (f32[512]{0:T(512)S(1)}, f32[512]{0:T(512)}, u32[]{:S(2)}) copy-start(f32[512]{0:T(512)} %param.11) | copy-start | bytes 6148
  45.0 20.1 %copy-start.5 = (f32[1024]{0:T(1024)S(1)}, f32[1024]{0:T(1024)}, u32[]{:S(2)}) copy-start(f32[1024]{0:T(1024)} %param.9) | copy-start | bytes 12292
  45.0 19.9 %all-to-all-start.1 = ((bf16[8,64,1024]{2,1,0:T(8,128)(2,1)}), bf16[8,64,1024]{2,1,0:T(8,128)(2,1)S(1)}, u32[]{:S(2)}, u32[]{:S(2)}) async-start(bf16[8,64,1024]{2,1,0:T(8,128)(2,1)} %bitcast.54), calls=%async_computation.1 | async-start | bytes 2097152 | tf_op jit(solution)/shard_map/all_to_all | solution.py:24
  50.1 0.7 collective-permute-start.1
  85.0 14.8 %all-to-all-start.2 = ((bf16[8,32,512]{2,1,0:T(8,128)(2,1)}), bf16[8,32,512]{2,1,0:T(8,128)(2,1)S(1)}, u32[]{:S(2)}, u32[]{:S(2)}) async-start(bf16[8,32,512]{2,1,0:T(8,128)(2,1)} %bitcast.4), calls=%async_computation.2 | async-start | bytes 524288 | tf_op jit(solution)/shard_map/all_to_all | solution.py:24
  89.8 18.6 %collective-permute-start.2 = (bf16[256,1024]{1,0:T(8,128)(2,1)S(1)}, bf16[256,1024]{1,0:T(8,128)(2,1)}, u32[]{:S(2)}, u32[]{:S(2)}) collective-permute-start(bf16[256,1024]{1,0:T(8,128)(2,1)S(1)} %all_gather.23), channel_id=1, source_target_pairs={{0,4},{4,0},{1,5},{5,1},{2,6},{6,2},{3,7},{7,3},{8,12},{12,8},{9,1... | collective-permute-start | bytes 1572872 | tf_op jit(solution)/shard_map/ppermute | solution.py:38
  100.6 38.4 %copy-start.1 = (bf16[1024,512]{1,0:T(8,128)(2,1)S(1)}, bf16[1024,512]{1,0:T(8,128)(2,1)}, u32[]{:S(2)}) copy-start(bf16[1024,512]{1,0:T(8,128)(2,1)} %param.10) | copy-start | bytes 3145732
  100.6 21.4 %all-to-all-start.3 = ((bf16[4,32,640]{2,1,0:T(8,128)(2,1)}), bf16[4,32,640]{2,1,0:T(8,128)(2,1)S(1)}, u32[]{:S(2)}, u32[]{:S(2)}) async-start(bf16[4,32,640]{2,1,0:T(8,128)(2,1)} %broadcast_in_dim.69), calls=%async_computation.3 | async-start | bytes 327680 | tf_op jit(solution)/shard_map/all_to_all | solution.py:24
  122.8 13.8 %all-to-all-start.4 = ((bf16[8,32,640]{2,1,0:T(8,128)(2,1)}), bf16[8,32,640]{2,1,0:T(8,128)(2,1)S(1)}, u32[]{:S(2)}, u32[]{:S(2)}) async-start(bf16[8,32,640]{2,1,0:T(8,128)(2,1)} %broadcast_in_dim.70), calls=%async_computation.4 | async-start | bytes 655360 | tf_op jit(solution)/shard_map/all_to_all | solution.py:24
  138.9 0.8 copy-start.2
  142.2 12.9 %all-to-all-start.5 = ((bf16[4,64,1024]{2,1,0:T(8,128)(2,1)}), bf16[4,64,1024]{2,1,0:T(8,128)(2,1)S(1)}, u32[]{:S(2)}, u32[]{:S(2)}) async-start(bf16[4,64,1024]{2,1,0:T(8,128)(2,1)} %bitcast.12), calls=%async_computation.5 | async-start | bytes 1048576 | tf_op jit(solution)/shard_map/all_to_all | solution.py:24
  146.7 8.4 %collective-permute-start.3 = (bf16[128,512]{1,0:T(8,128)(2,1)S(1)}, bf16[128,512]{1,0:T(8,128)(2,1)S(1)}, u32[]{:S(2)}, u32[]{:S(2)}) collective-permute-start(bf16[128,512]{1,0:T(8,128)(2,1)S(1)} %dynamic-slice_bitcast_fusion.2), channel_id=1, source_target_pairs={{0,4},{4,0},{1,5},{5,1},{2,6},{6,2},{3,7},{7,3},{8,12},{12,8},{9,1... | collective-permute-start | bytes 393224 | tf_op jit(solution)/shard_map/ppermute | solution.py:38
  156.5 20.3 %all-to-all-start.6 = ((bf16[8,72,1024]{2,1,0:T(8,128)(2,1)}), bf16[8,72,1024]{2,1,0:T(8,128)(2,1)S(1)}, u32[]{:S(2)}, u32[]{:S(2)}) async-start(bf16[8,72,1024]{2,1,0:T(8,128)(2,1)} %broadcast_in_dim.76), calls=%async_computation.6 | async-start | bytes 2359296 | tf_op jit(solution)/shard_map/all_to_all | solution.py:24
  167.3 10.8 %copy-start.4 = (bf16[512,512]{1,0:T(8,128)(2,1)S(1)}, bf16[512,512]{1,0:T(8,128)(2,1)}, u32[]{:S(2)}) copy-start(bf16[512,512]{1,0:T(8,128)(2,1)} %copy-done.3) | copy-start | bytes 1572868

commit v4 on v3

--- a/solution.py
+++ b/solution.py
@@ -76,19 +76,20 @@
     my_target = lax.ppermute(
         targets.astype(f32) - dec_bias, ("c", "xh"), [(0, 0), (1, 2), (2, 1), (3, 3)]
     )
-    pre_parts, my_target = together(pre_parts, my_target)
+    same = c == xh
+    dec_pair = jnp.where(
+        same, jnp.stack([dec_weight, dec_other]), jnp.stack([dec_other, dec_weight])
+    )
+    pre_parts, my_target, dec_pair = together(pre_parts, my_target, dec_pair)
     preact = jnp.sum(pre_parts.astype(f32), axis=0) + enc_bias
     lifted = jnp.maximum(preact, 0.0)
     latent = lifted * lifted
     latent_sum = fold(latent)
     latent_low = lax.all_gather(latent.astype(bf16), "y", axis=0, tiled=True)
 
-    same = c == xh
-    recon_mine = dot(latent_low, dec_weight, 1, 0)
-    recon_other = dot(latent_low, dec_other, 1, 0)
-    send = jnp.where(same, recon_other, recon_mine).astype(bf16)
+    send = dot(latent_low, dec_pair[1], 1, 0).astype(bf16)
     both = lax.all_gather(send, "c", axis=0, tiled=False)
-    part = jnp.where(same, recon_mine, recon_other) + pick(both, 1 - c).astype(f32)
+    part = dot(latent_low, dec_pair[0], 1, 0) + pick(both, 1 - c).astype(f32)
     part = jnp.sum(exchange(part.astype(bf16), ("xl", "zl"), XL * ZL).astype(f32), axis=0)
     block = lax.broadcasted_iota(jnp.int32, (ZH, rows, width), 0)
     minus = jnp.where(block == zh, my_target[None], 0.0).reshape(ZH * rows, width)

time: 183 us -> 182 us (level)
  matrix products: 12.6 us -> 9.63 us
  local copies, waits for them, and re-layouts: 4.55 us -> 7.35 us
  waiting for transfers between devices: 57.7 us -> 55 us
    all_to_all x6, waiting for transfers between devices: 53.5 us -> 49.8 us  [exchange(): parts = lax.all_to_all(x, axes, 0, 0, tiled=True)]
    select_n x0 -> x1, other arithmetic: none -> 3.24 us  [local(): jnp.where(same, jnp.stack([dec_weight, dec_other]), jnp.stack([dec_other,...]
    dot_general x8, matrix products: 12.6 us -> 9.63 us  [dot(): lax.dot_general(a, b, (((da,), (db,)), ((), ())), preferred_element_type=...]
    unnamed x16 -> x32, local copies, waits for them, and re-layouts: 0.32 us -> 3.11 us
  transfers between devices with their start and end apart: 10 -> 10, of which waited for: 7 -> 7; matrix products, arithmetic and copies ran while one was open for 4% -> 5% of each run, Pallas kernels for 0% -> 0%
where the time goes in v4:
time: 182 us; the launch traced here: 181 us
  blocking collectives  57 us (31%)
  waiting for transfers between devices  55 us (30%)
  starting transfers between devices  41.3 us (23%)
  matrix products  9.63 us (5%)
  local copies, waits for them, and re-layouts  7.35 us (4%)
  other arithmetic  5.95 us (3%)
  between operations  4.69 us (3%)
    all_to_all x6, waiting for transfers between devices, exchange(): parts = lax.all_to_all(x, axes, 0, 0, tiled=True)  49.8 us
    all_to_all x6, starting transfers between devices, exchange(): parts = lax.all_to_all(x, axes, 0, 0, tiled=True)  29.3 us
    all_to_all x1, blocking collectives, exchange(): parts = lax.all_to_all(x, axes, 0, 0, tiled=True)  29.1 us
    all_gather x1, blocking collectives, local(): latent_low = lax.all_gather(latent.astype(bf16), 'y', axis=0, tiled=True)  13.6 us
    ppermute x3, starting transfers between devices, partner(): return lax.ppermute(x, 'xh', SWAP)  11.3 us
    dot_general x8, matrix products, dot(): lax.dot_general(a, b, (((da,), (db,)), ((), ())), preferred_element_type=...  9.63 us
    all_gather x1, blocking collectives, local(): x = lax.all_gather(x, 'xl', axis=0, tiled=True)  5.63 us
    ppermute x3, waiting for transfers between devices, partner(): return lax.ppermute(x, 'xh', SWAP)  5.25 us
  transfers between devices with their start and end apart: 10, of which 7 were waited for; matrix products, arithmetic and copies ran while one was open for 5% of the time, Pallas kernels for 0%

profile of v4, /device:TPU:8, one launch (start us, length us, event | category | flops | bytes accessed | tf_op | source)
XLA Modules:
  0.0 180.9 jit_solution(12951063305822860258)
XLA Ops:
  0.6 5.1 %collective-permute-start = (bf16[1024,512]{1,0:T(8,128)(2,1)}, bf16[1024,512]{1,0:T(8,128)(2,1)S(1)}, u32[]{:S(2)}, u32[]{:S(2)}) collective-permute-start(bf16[1024,512]{1,0:T(8,128)(2,1)} %param.10), channel_id=1, source_target_pairs={{0,4},{4,0},{1,5},{5,1},{2,6},{6,2},{3,7},{7,3},{8,12},{12,8},{9,1... | collective-permute-start | bytes 3145736 | tf_op jit(solution)/shard_map/ppermute | solution.py:38
  5.7 0.7 broadcast_in_dim.65
  6.4 29.1 %all_to_all.54 = bf16[16,8,512]{2,1,0:T(8,128)(2,1)S(1)} all-to-all(bf16[16,8,512]{2,1,0:T(8,128)(2,1)S(1)} %broadcast_in_dim.65), channel_id=1, replica_groups=mesh['zh'=4,'zl'=4,'xl'=2,'c'=2,'xh'=2,'y'=4] {'zl','zh'}, dimensions={0} | all-to-all | bytes 262144 | tf_op jit(solution)/shard_map/all_to_all | solution.py:24
  35.5 5.6 %all_gather.21 = bf16[256,512]{1,0:T(8,128)(2,1)S(1)} all-gather(bf16[128,512]{1,0:T(8,128)(2,1)S(1)} %bitcast.64), channel_id=1, replica_groups=mesh['zh'=4,'zl'=4,'xl'=2,'c'=2,'xh'=2,'y'=4] {'xl'}, dimensions={0}, use_global_device_ids=true | all-gather | bytes 393216 | tf_op jit(solution)/shard_map/all_gather | solution.py:71
  41.2 1.0 copy-done.2
  42.1 2.2 %all_gather.22 = bf16[512,512]{1,0:T(8,128)(2,1)S(1)} all-gather(bf16[256,512]{1,0:T(8,128)(2,1)S(1)} %all_gather.21), channel_id=1, replica_groups=mesh['zh'=4,'zl'=4,'xl'=2,'c'=2,'xh'=2,'y'=4] {'c'}, dimensions={0}, use_global_device_ids=true | all-gather | bytes 786432 | tf_op jit(solution)/shard_map/all_gather | solution.py:73
  44.3 0.8 copy-done.9
  45.1 1.7 convolution_convert_fusion.1
  46.8 4.9 %all-to-all-start.1 = ((bf16[8,64,1024]{2,1,0:T(8,128)(2,1)}), bf16[8,64,1024]{2,1,0:T(8,128)(2,1)S(1)}, u32[]{:S(2)}, u32[]{:S(2)}) async-start(bf16[8,64,1024]{2,1,0:T(8,128)(2,1)} %bitcast.61), calls=%async_computation.1 | async-start | bytes 2097152 | tf_op jit(solution)/shard_map/all_to_all | solution.py:24
  51.7 0.7 collective-permute-start.1
  52.4 3.2 %maximum_select_fusion = bf16[2,1024,512]{2,1,0:T(8,128)(2,1)} fusion(bf16[1,1024,512]{2,1,0:T(8,128)(2,1)} %bitcast.59, bf16[1,1024,512]{2,1,0:T(8,128)(2,1)S(1)} %bitcast.58, pred[]{:T(512)S(6)} %eq.38), kind=kLoop, calls=%fused_computation | loop fusion | flops 3145728 | bytes 4194305 | tf_op jit(solution)/shard_map/jit(_where)/select_n | solution.py:80
  55.7 10.9 %all-to-all-done.1 = bf16[8,64,1024]{2,1,0:T(8,128)(2,1)S(1)} async-done(((bf16[8,64,1024]{2,1,0:T(8,128)(2,1)}), bf16[8,64,1024]{2,1,0:T(8,128)(2,1)S(1)}, u32[]{:S(2)}, u32[]{:S(2)}) %all-to-all-start.1) | async-done | bytes 1048608 | tf_op jit(solution)/shard_map/all_to_all | solution.py:24
  66.6 0.2 convert_reduce_fusion
  66.8 13.6 %all_gather.23 = bf16[256,1024]{1,0:T(8,128)(2,1)S(1)} all-gather(bf16[64,1024]{1,0:T(8,128)(2,1)S(1)} %multiply_convert_fusion), channel_id=1, replica_groups=mesh['zh'=4,'zl'=4,'xl'=2,'c'=2,'xh'=2,'y'=4] {'y'}, dimensions={0}, use_global_device_ids=true | all-gather | bytes 655360 | tf_op jit(solution)/shard_map/all_gather | solution.py:88
  80.4 0.4 convolution_convert_fusion.2
  80.8 2.2 %all-gather = bf16[512,512]{1,0:T(8,128)(2,1)S(1)} all-gather(bf16[256,512]{1,0:T(8,128)(2,1)S(1)} %convolution_convert_fusion.2), channel_id=2, replica_groups=mesh['zh'=4,'zl'=4,'xl'=2,'c'=2,'xh'=2,'y'=4] {'c'}, dimensions={0}, use_global_device_ids=true | all-gather | bytes 786432 | tf_op jit(solution)/shard_map/all_gather | solution.py:91
  83.0 1.1 fusion.1
  84.2 4.7 %all-to-all-start.2 = ((bf16[8,32,512]{2,1,0:T(8,128)(2,1)}), bf16[8,32,512]{2,1,0:T(8,128)(2,1)S(1)}, u32[]{:S(2)}, u32[]{:S(2)}) async-start(bf16[8,32,512]{2,1,0:T(8,128)(2,1)} %bitcast.8), calls=%async_computation.2 | async-start | bytes 524288 | tf_op jit(solution)/shard_map/all_to_all | solution.py:24
  88.9 0.1 iota.30
  89.0 3.7 %collective-permute-start.2 = (bf16[256,1024]{1,0:T(8,128)(2,1)S(1)}, bf16[256,1024]{1,0:T(8,128)(2,1)}, u32[]{:S(2)}, u32[]{:S(2)}) collective-permute-start(bf16[256,1024]{1,0:T(8,128)(2,1)S(1)} %all_gather.23), channel_id=1, source_target_pairs={{0,4},{4,0},{1,5},{5,1},{2,6},{6,2},{3,7},{7,3},{8,12},{12,8},{9,1... | collective-permute-start | bytes 1572872 | tf_op jit(solution)/shard_map/ppermute | solution.py:38
  92.8 6.1 %all-to-all-done.2 = bf16[8,32,512]{2,1,0:T(8,128)(2,1)S(1)} async-done(((bf16[8,32,512]{2,1,0:T(8,128)(2,1)}), bf16[8,32,512]{2,1,0:T(8,128)(2,1)S(1)}, u32[]{:S(2)}, u32[]{:S(2)}) %all-to-all-start.2) | async-done | bytes 262176 | tf_op jit(solution)/shard_map/all_to_all | solution.py:24
  99.1 0.7 broadcast_in_dim.69
  99.7 6.5 %all-to-all-start.3 = ((bf16[4,32,640]{2,1,0:T(8,128)(2,1)}), bf16[4,32,640]{2,1,0:T(8,128)(2,1)S(1)}, u32[]{:S(2)}, u32[]{:S(2)}) async-start(bf16[4,32,640]{2,1,0:T(8,128)(2,1)} %broadcast_in_dim.69), calls=%async_computation.3 | async-start | bytes 327680 | tf_op jit(solution)/shard_map/all_to_all | solution.py:24
  106.2 1.4 collective-permute-done.2
  107.6 13.4 %all-to-all-done.3 = bf16[4,32,640]{2,1,0:T(8,128)(2,1)S(1)} async-done(((bf16[4,32,640]{2,1,0:T(8,128)(2,1)}), bf16[4,32,640]{2,1,0:T(8,128)(2,1)S(1)}, u32[]{:S(2)}, u32[]{:S(2)}) %all-to-all-start.3) | async-done | bytes 163872 | tf_op jit(solution)/shard_map/all_to_all | solution.py:24
  121.1 0.8 broadcast_in_dim.70
  121.9 3.5 %all-to-all-start.4 = ((bf16[8,32,640]{2,1,0:T(8,128)(2,1)}), bf16[8,32,640]{2,1,0:T(8,128)(2,1)S(1)}, u32[]{:S(2)}, u32[]{:S(2)}) async-start(bf16[8,32,640]{2,1,0:T(8,128)(2,1)} %broadcast_in_dim.70), calls=%async_computation.4 | async-start | bytes 655360 | tf_op jit(solution)/shard_map/all_to_all | solution.py:24
  125.4 10.2 %all-to-all-done.4 = bf16[8,32,640]{2,1,0:T(8,128)(2,1)S(1)} async-done(((bf16[8,32,640]{2,1,0:T(8,128)(2,1)}), bf16[8,32,640]{2,1,0:T(8,128)(2,1)S(1)}, u32[]{:S(2)}, u32[]{:S(2)}) %all-to-all-start.4) | async-done | bytes 327712 | tf_op jit(solution)/shard_map/all_to_all | solution.py:24
  135.6 2.4 %all_gather.26 = bf16[2,256,640]{2,1,0:T(8,128)(2,1)S(1)} all-gather(bf16[1,256,640]{2,1,0:T(8,128)(2,1)S(1)} %bitcast.60), channel_id=1, replica_groups=mesh['zh'=4,'zl'=4,'xl'=2,'c'=2,'xh'=2,'y'=4] {'c'}, dimensions={0}, use_global_device_ids=true | all-gather | bytes 983040 | tf_op jit(solution)/shard_map/all_gather | solution.py:103
  138.1 0.5 fusion.11
  138.6 0.3 copy-done.4
  138.9 1.3 fusion
  140.1 4.5 %all-to-all-start.5 = ((bf16[4,64,1024]{2,1,0:T(8,128)(2,1)}), bf16[4,64,1024]{2,1,0:T(8,128)(2,1)S(1)}, u32[]{:S(2)}, u32[]{:S(2)}) async-start(bf16[4,64,1024]{2,1,0:T(8,128)(2,1)} %bitcast.16), calls=%async_computation.5 | async-start | bytes 1048576 | tf_op jit(solution)/shard_map/all_to_all | solution.py:24
  144.7 2.5 %collective-permute-start.3 = (bf16[128,512]{1,0:T(8,128)(2,1)S(1)}, bf16[128,512]{1,0:T(8,128)(2,1)S(1)}, u32[]{:S(2)}, u32[]{:S(2)}) collective-permute-start(bf16[128,512]{1,0:T(8,128)(2,1)S(1)} %dynamic-slice_bitcast_fusion.2), channel_id=1, source_target_pairs={{0,4},{4,0},{1,5},{5,1},{2,6},{6,2},{3,7},{7,3},{8,12},{12,8},{9,1... | collective-permute-start | bytes 393224 | tf_op jit(solution)/shard_map/ppermute | solution.py:38
  147.2 0.7 convert_reduce_fusion.7
  149.2 3.8 %collective-permute-done.3 = bf16[128,512]{1,0:T(8,128)(2,1)S(1)} collective-permute-done((bf16[128,512]{1,0:T(8,128)(2,1)S(1)}, bf16[128,512]{1,0:T(8,128)(2,1)S(1)}, u32[]{:S(2)}, u32[]{:S(2)}) %collective-permute-start.3) | collective-permute-done | bytes 131104 | tf_op jit(solution)/shard_map/ppermute | solution.py:38
  153.0 0.7 copy-done.11
  154.0 1.2 broadcast_in_dim.76
  155.2 5.2 %all-to-all-start.6 = ((bf16[8,72,1024]{2,1,0:T(8,128)(2,1)}), bf16[8,72,1024]{2,1,0:T(8,128)(2,1)S(1)}, u32[]{:S(2)}, u32[]{:S(2)}) async-start(bf16[8,72,1024]{2,1,0:T(8,128)(2,1)} %broadcast_in_dim.76), calls=%async_computation.6 | async-start | bytes 2359296 | tf_op jit(solution)/shard_map/all_to_all | solution.py:24
  160.4 0.5 fusion.9
  160.8 0.4 copy-done.12
  161.2 2.0 %all_gather.27 = bf16[256,512]{1,0:T(8,128)(2,1)S(1)} all-gather(bf16[128,512]{1,0:T(8,128)(2,1)S(1)} %copy-done.12), channel_id=1, replica_groups=mesh['zh'=4,'zl'=4,'xl'=2,'c'=2,'xh'=2,'y'=4] {'c'}, dimensions={0}, use_global_device_ids=true | all-gather | bytes 393216 | tf_op jit(solution)/shard_map/all_gather | solution.py:111
  163.3 0.6 add.118
  163.8 2.5 %add_convert_fusion = bf16[1024,512]{1,0:T(8,128)(2,1)} fusion(f32[1024,512]{1,0:T(8,128)S(1)} %fusion.9, bf16[256,1024]{1,0:T(8,128)(2,1)} %collective-permute-done.2, bf16[256,512]{1,0:T(8,128)(2,1)S(1)} %all_gather.27), kind=kOutput, calls=%fused_computation.1 | convolution fusion | flops 269484032 | bytes 3932160 | tf_op jit(solution)/shard_map/dot_general | solution.py:20
  166.3 9.1 %all-to-all-done.6 = bf16[8,72,1024]{2,1,0:T(8,128)(2,1)S(1)} async-done(((bf16[8,72,1024]{2,1,0:T(8,128)(2,1)}), bf16[8,72,1024]{2,1,0:T(8,128)(2,1)S(1)}, u32[]{:S(2)}, u32[]{:S(2)}) %all-to-all-start.6) | async-done | bytes 1179680 | tf_op jit(solution)/shard_map/all_to_all | solution.py:24
  175.5 0.6 fusion.23
  176.1 0.6 slice_add_fusion
  176.8 1.7 convolution_convert_fusion
  (60 shorter events, 1.0 us)
Async XLA Ops:
  0.6 44.5 %copy-start = (bf16[512,1024]{1,0:T(8,128)(2,1)S(1)}, bf16[512,1024]{1,0:T(8,128)(2,1)}, u32[]{:S(2)}) copy-start(bf16[512,1024]{1,0:T(8,128)(2,1)} %param.8) | copy-start | bytes 3145732
  0.6 40.5 %collective-permute-start = (bf16[1024,512]{1,0:T(8,128)(2,1)}, bf16[1024,512]{1,0:T(8,128)(2,1)S(1)}, u32[]{:S(2)}, u32[]{:S(2)}) collective-permute-start(bf16[1024,512]{1,0:T(8,128)(2,1)} %param.10), channel_id=1, source_target_pairs={{0,4},{4,0},{1,5},{5,1},{2,6},{6,2},{3,7},{7,3},{8,12},{12,8},{9,1... | collective-permute-start | bytes 3145736 | tf_op jit(solution)/shard_map/ppermute | solution.py:38
  41.2 1.0 copy-start.2
  44.3 0.8 copy-start.9
  45.1 6.6 %copy-start.14 = (bf16[8,512]{1,0:T(8,128)(2,1)S(1)}, bf16[8,512]{1,0:T(8,128)(2,1)}, u32[]{:S(2)}) copy-start(bf16[8,512]{1,0:T(8,128)(2,1)} %param.7) | copy-start | bytes 24580
  45.1 6.6 %copy-start.15 = (f32[512]{0:T(512)S(1)}, f32[512]{0:T(512)}, u32[]{:S(2)}) copy-start(f32[512]{0:T(512)} %param.11) | copy-start | bytes 6148
  45.1 7.3 %copy-start.1 = (bf16[1024,512]{1,0:T(8,128)(2,1)S(1)}, bf16[1024,512]{1,0:T(8,128)(2,1)}, u32[]{:S(2)}) copy-start(bf16[1024,512]{1,0:T(8,128)(2,1)} %param.10) | copy-start | bytes 3145732
  46.8 19.8 %all-to-all-start.1 = ((bf16[8,64,1024]{2,1,0:T(8,128)(2,1)}), bf16[8,64,1024]{2,1,0:T(8,128)(2,1)S(1)}, u32[]{:S(2)}, u32[]{:S(2)}) async-start(bf16[8,64,1024]{2,1,0:T(8,128)(2,1)} %bitcast.61), calls=%async_computation.1 | async-start | bytes 2097152 | tf_op jit(solution)/shard_map/all_to_all | solution.py:24
  51.7 3.9 %collective-permute-start.1 = (f32[8,512]{1,0:T(8,128)S(1)}, f32[8,512]{1,0:T(8,128)S(1)}, u32[]{:S(2)}, u32[]{:S(2)}) collective-permute-start(f32[8,512]{1,0:T(8,128)S(1)} %convert_subtract_fusion), channel_id=1, source_target_pairs={{0,0},{4,8},{8,4},{12,12},{1,1},{5,9},{9,5},{13,13},{2,2},{6,10},{... | collective-permute-start | bytes 49160 | tf_op jit(solution)/shard_map/ppermute | solution.py:76
  52.4 14.3 %copy-start.13 = (f32[1024]{0:T(1024)S(1)}, f32[1024]{0:T(1024)}, u32[]{:S(2)}) copy-start(f32[1024]{0:T(1024)} %param.9) | copy-start | bytes 12292
  66.6 13.8 %copy-start.6 = (bf16[2,1024,512]{2,1,0:T(8,128)(2,1)S(1)}, bf16[2,1024,512]{2,1,0:T(8,128)(2,1)}, u32[]{:S(2)}) copy-start(bf16[2,1024,512]{2,1,0:T(8,128)(2,1)} %maximum_select_fusion) | copy-start | bytes 6291460
  80.4 8.6 %copy-start.7 = (bf16[256,1024]{1,0:T(8,128)(2,1)}, bf16[256,1024]{1,0:T(8,128)(2,1)S(1)}, u32[]{:S(2)}) copy-start(bf16[256,1024]{1,0:T(8,128)(2,1)S(1)} %all_gather.23) | copy-start | bytes 1572868
  84.2 14.8 %all-to-all-start.2 = ((bf16[8,32,512]{2,1,0:T(8,128)(2,1)}), bf16[8,32,512]{2,1,0:T(8,128)(2,1)S(1)}, u32[]{:S(2)}, u32[]{:S(2)}) async-start(bf16[8,32,512]{2,1,0:T(8,128)(2,1)} %bitcast.8), calls=%async_computation.2 | async-start | bytes 524288 | tf_op jit(solution)/shard_map/all_to_all | solution.py:24
  89.0 18.6 %collective-permute-start.2 = (bf16[256,1024]{1,0:T(8,128)(2,1)S(1)}, bf16[256,1024]{1,0:T(8,128)(2,1)}, u32[]{:S(2)}, u32[]{:S(2)}) collective-permute-start(bf16[256,1024]{1,0:T(8,128)(2,1)S(1)} %all_gather.23), channel_id=1, source_target_pairs={{0,4},{4,0},{1,5},{5,1},{2,6},{6,2},{3,7},{7,3},{8,12},{12,8},{9,1... | collective-permute-start | bytes 1572872 | tf_op jit(solution)/shard_map/ppermute | solution.py:38
  99.7 21.3 %all-to-all-start.3 = ((bf16[4,32,640]{2,1,0:T(8,128)(2,1)}), bf16[4,32,640]{2,1,0:T(8,128)(2,1)S(1)}, u32[]{:S(2)}, u32[]{:S(2)}) async-start(bf16[4,32,640]{2,1,0:T(8,128)(2,1)} %broadcast_in_dim.69), calls=%async_computation.3 | async-start | bytes 327680 | tf_op jit(solution)/shard_map/all_to_all | solution.py:24
  121.9 13.8 %all-to-all-start.4 = ((bf16[8,32,640]{2,1,0:T(8,128)(2,1)}), bf16[8,32,640]{2,1,0:T(8,128)(2,1)S(1)}, u32[]{:S(2)}, u32[]{:S(2)}) async-start(bf16[8,32,640]{2,1,0:T(8,128)(2,1)} %broadcast_in_dim.70), calls=%async_computation.4 | async-start | bytes 655360 | tf_op jit(solution)/shard_map/all_to_all | solution.py:24
  135.6 3.2 %copy-start.3 = (bf16[1024,512]{1,0:T(8,128)(2,1)S(1)}, bf16[1024,512]{1,0:T(8,128)(2,1)}, u32[]{:S(2)}) copy-start(bf16[1024,512]{1,0:T(8,128)(2,1)} %copy-done.2) | copy-start | bytes 3145732
  138.1 0.7 copy-start.4
  140.1 13.6 %all-to-all-start.5 = ((bf16[4,64,1024]{2,1,0:T(8,128)(2,1)}), bf16[4,64,1024]{2,1,0:T(8,128)(2,1)S(1)}, u32[]{:S(2)}, u32[]{:S(2)}) async-start(bf16[4,64,1024]{2,1,0:T(8,128)(2,1)} %bitcast.16), calls=%async_computation.5 | async-start | bytes 1048576 | tf_op jit(solution)/shard_map/all_to_all | solution.py:24
  144.7 8.4 %collective-permute-start.3 = (bf16[128,512]{1,0:T(8,128)(2,1)S(1)}, bf16[128,512]{1,0:T(8,128)(2,1)S(1)}, u32[]{:S(2)}, u32[]{:S(2)}) collective-permute-start(bf16[128,512]{1,0:T(8,128)(2,1)S(1)} %dynamic-slice_bitcast_fusion.2), channel_id=1, source_target_pairs={{0,4},{4,0},{1,5},{5,1},{2,6},{6,2},{3,7},{7,3},{8,12},{12,8},{9,1... | collective-permute-start | bytes 393224 | tf_op jit(solution)/shard_map/ppermute | solution.py:38
  153.0 0.7 copy-start.11
  153.9 6.5 %copy-start.5 = (bf16[256,640]{1,0:T(8,128)(2,1)S(1)}, bf16[256,640]{1,0:T(8,128)(2,1)}, u32[]{:S(2)}) copy-start(bf16[256,640]{1,0:T(8,128)(2,1)} %copy-done.4) | copy-start | bytes 983044
  154.0 6.4 %copy-start.8 = (bf16[256,1024]{1,0:T(8,128)(2,1)S(1)}, bf16[256,1024]{1,0:T(8,128)(2,1)}, u32[]{:S(2)}) copy-start(bf16[256,1024]{1,0:T(8,128)(2,1)} %copy-done.7) | copy-start | bytes 1572868
  155.2 20.3 %all-to-all-start.6 = ((bf16[8,72,1024]{2,1,0:T(8,128)(2,1)}), bf16[8,72,1024]{2,1,0:T(8,128)(2,1)S(1)}, u32[]{:S(2)}, u32[]{:S(2)}) async-start(bf16[8,72,1024]{2,1,0:T(8,128)(2,1)} %broadcast_in_dim.76), calls=%async_computation.6 | async-start | bytes 2359296 | tf_op jit(solution)/shard_map/all_to_all | solution.py:24
  160.3 0.9 copy-start.12
  175.4 1.3 copy-start.10

commit v5 on v4

--- a/solution.py
+++ b/solution.py
@@ -69,8 +69,8 @@
     dec_other = partner(dec_weight)
     x = share(inputs, ("zl", "zh"), ZL * ZH).reshape(-1, width)
     x = lax.all_gather(x, "xl", axis=0, tiled=True)
-    x, dec_other = together(x, dec_other)
     every_row = lax.all_gather(x, "c", axis=0, tiled=True)
+    every_row, dec_other = together(every_row, dec_other)
     pre = dot(every_row, enc_weight, 1, 0).astype(bf16)
     pre_parts = exchange(pre, TOK, N_TOK)
     my_target = lax.ppermute(

time: 182 us -> 183 us (level)
  transfers between devices with their start and end apart: 10 -> 10, of which waited for: 7 -> 7; matrix products, arithmetic and copies ran while one was open for 5% -> 6% of each run, Pallas kernels for 0% -> 0%
where the time goes in v5:
time: 183 us; the launch traced here: 182 us
  blocking collectives  56.9 us (31%)
  waiting for transfers between devices  54.1 us (30%)
  starting transfers between devices  41.2 us (23%)
  matrix products  10.9 us (6%)
  local copies, waits for them, and re-layouts  7.07 us (4%)
  other arithmetic  6.88 us (4%)
  between operations  4.57 us (2%)
    all_to_all x6, waiting for transfers between devices, exchange(): parts = lax.all_to_all(x, axes, 0, 0, tiled=True)  49.7 us
    all_to_all x6, starting transfers between devices, exchange(): parts = lax.all_to_all(x, axes, 0, 0, tiled=True)  29.3 us
    all_to_all x1, blocking collectives, exchange(): parts = lax.all_to_all(x, axes, 0, 0, tiled=True)  29.1 us
    all_gather x1, blocking collectives, local(): latent_low = lax.all_gather(latent.astype(bf16), 'y', axis=0, tiled=True)  13.6 us
    ppermute x3, starting transfers between devices, partner(): return lax.ppermute(x, 'xh', SWAP)  11.3 us
    dot_general x8, matrix products, dot(): lax.dot_general(a, b, (((da,), (db,)), ((), ())), preferred_element_type=...  10.9 us
    all_gather x1, blocking collectives, local(): x = lax.all_gather(x, 'xl', axis=0, tiled=True)  5.63 us
    ppermute x3, waiting for transfers between devices, partner(): return lax.ppermute(x, 'xh', SWAP)  4.36 us
  transfers between devices with their start and end apart: 10, of which 7 were waited for; matrix products, arithmetic and copies ran while one was open for 6% of the time, Pallas kernels for 0%

profile of v5, /device:TPU:8, one launch (start us, length us, event | category | flops | bytes accessed | tf_op | source)
XLA Modules:
  0.0 181.6 jit_solution(15043491502465926600)
XLA Ops:
  0.6 5.1 %collective-permute-start = (bf16[1024,512]{1,0:T(8,128)(2,1)}, bf16[1024,512]{1,0:T(8,128)(2,1)}, u32[]{:S(2)}, u32[]{:S(2)}) collective-permute-start(bf16[1024,512]{1,0:T(8,128)(2,1)} %param.10), channel_id=1, source_target_pairs={{0,4},{4,0},{1,5},{5,1},{2,6},{6,2},{3,7},{7,3},{8,12},{12,8},{9,1... | collective-permute-start | bytes 3145736 | tf_op jit(solution)/shard_map/ppermute | solution.py:38
  5.7 0.7 broadcast_in_dim.65
  6.4 29.1 %all_to_all.54 = bf16[16,8,512]{2,1,0:T(8,128)(2,1)S(1)} all-to-all(bf16[16,8,512]{2,1,0:T(8,128)(2,1)S(1)} %broadcast_in_dim.65), channel_id=1, replica_groups=mesh['zh'=4,'zl'=4,'xl'=2,'c'=2,'xh'=2,'y'=4] {'zl','zh'}, dimensions={0} | all-to-all | bytes 262144 | tf_op jit(solution)/shard_map/all_to_all | solution.py:24
  35.5 5.6 %all_gather.21 = bf16[256,512]{1,0:T(8,128)(2,1)S(1)} all-gather(bf16[128,512]{1,0:T(8,128)(2,1)S(1)} %bitcast.63), channel_id=1, replica_groups=mesh['zh'=4,'zl'=4,'xl'=2,'c'=2,'xh'=2,'y'=4] {'xl'}, dimensions={0}, use_global_device_ids=true | all-gather | bytes 393216 | tf_op jit(solution)/shard_map/all_gather | solution.py:71
  41.2 2.2 %all_gather.22 = bf16[512,512]{1,0:T(8,128)(2,1)S(1)} all-gather(bf16[256,512]{1,0:T(8,128)(2,1)S(1)} %all_gather.21), channel_id=1, replica_groups=mesh['zh'=4,'zl'=4,'xl'=2,'c'=2,'xh'=2,'y'=4] {'c'}, dimensions={0}, use_global_device_ids=true | all-gather | bytes 786432 | tf_op jit(solution)/shard_map/all_gather | solution.py:72
  43.3 0.8 copy-done.8
  44.1 1.7 convolution_convert_fusion.1
  45.8 4.9 %all-to-all-start.1 = ((bf16[8,64,1024]{2,1,0:T(8,128)(2,1)}), bf16[8,64,1024]{2,1,0:T(8,128)(2,1)S(1)}, u32[]{:S(2)}, u32[]{:S(2)}) async-start(bf16[8,64,1024]{2,1,0:T(8,128)(2,1)} %bitcast.60), calls=%async_computation.1 | async-start | bytes 2097152 | tf_op jit(solution)/shard_map/all_to_all | solution.py:24
  50.7 0.7 collective-permute-start.1
  51.4 3.3 %maximum_select_fusion = bf16[2,1024,512]{2,1,0:T(8,128)(2,1)} fusion(bf16[1,1024,512]{2,1,0:T(8,128)(2,1)} %bitcast.3, bf16[1,1024,512]{2,1,0:T(8,128)(2,1)S(1)} %bitcast.58, pred[]{:T(512)S(6)} %eq.38), kind=kLoop, calls=%fused_computation | loop fusion | flops 3145728 | bytes 4194305 | tf_op jit(solution)/shard_map/jit(_where)/select_n | solution.py:80
  54.7 10.9 %all-to-all-done.1 = bf16[8,64,1024]{2,1,0:T(8,128)(2,1)S(1)} async-done(((bf16[8,64,1024]{2,1,0:T(8,128)(2,1)}), bf16[8,64,1024]{2,1,0:T(8,128)(2,1)S(1)}, u32[]{:S(2)}, u32[]{:S(2)}) %all-to-all-start.1) | async-done | bytes 1048608 | tf_op jit(solution)/shard_map/all_to_all | solution.py:24
  65.6 0.2 convert_reduce_fusion
  65.8 13.6 %all_gather.23 = bf16[256,1024]{1,0:T(8,128)(2,1)S(1)} all-gather(bf16[64,1024]{1,0:T(8,128)(2,1)S(1)} %multiply_convert_fusion), channel_id=1, replica_groups=mesh['zh'=4,'zl'=4,'xl'=2,'c'=2,'xh'=2,'y'=4] {'y'}, dimensions={0}, use_global_device_ids=true | all-gather | bytes 655360 | tf_op jit(solution)/shard_map/all_gather | solution.py:88
  79.4 0.4 convolution_convert_fusion.2
  79.8 2.2 %all-gather = bf16[512,512]{1,0:T(8,128)(2,1)S(1)} all-gather(bf16[256,512]{1,0:T(8,128)(2,1)S(1)} %convolution_convert_fusion.2), channel_id=2, replica_groups=mesh['zh'=4,'zl'=4,'xl'=2,'c'=2,'xh'=2,'y'=4] {'c'}, dimensions={0}, use_global_device_ids=true | all-gather | bytes 786432 | tf_op jit(solution)/shard_map/all_gather | solution.py:91
  82.0 1.1 fusion.1
  83.2 4.7 %all-to-all-start.2 = ((bf16[8,32,512]{2,1,0:T(8,128)(2,1)}), bf16[8,32,512]{2,1,0:T(8,128)(2,1)S(1)}, u32[]{:S(2)}, u32[]{:S(2)}) async-start(bf16[8,32,512]{2,1,0:T(8,128)(2,1)} %bitcast.8), calls=%async_computation.2 | async-start | bytes 524288 | tf_op jit(solution)/shard_map/all_to_all | solution.py:24
  87.9 0.1 iota.30
  88.0 3.7 %collective-permute-start.2 = (bf16[256,1024]{1,0:T(8,128)(2,1)S(1)}, bf16[256,1024]{1,0:T(8,128)(2,1)}, u32[]{:S(2)}, u32[]{:S(2)}) collective-permute-start(bf16[256,1024]{1,0:T(8,128)(2,1)S(1)} %all_gather.23), channel_id=1, source_target_pairs={{0,4},{4,0},{1,5},{5,1},{2,6},{6,2},{3,7},{7,3},{8,12},{12,8},{9,1... | collective-permute-start | bytes 1572872 | tf_op jit(solution)/shard_map/ppermute | solution.py:38
  91.8 6.1 %all-to-all-done.2 = bf16[8,32,512]{2,1,0:T(8,128)(2,1)S(1)} async-done(((bf16[8,32,512]{2,1,0:T(8,128)(2,1)}), bf16[8,32,512]{2,1,0:T(8,128)(2,1)S(1)}, u32[]{:S(2)}, u32[]{:S(2)}) %all-to-all-start.2) | async-done | bytes 262176 | tf_op jit(solution)/shard_map/all_to_all | solution.py:24
  98.1 0.7 broadcast_in_dim.69
  98.7 6.5 %all-to-all-start.3 = ((bf16[4,32,640]{2,1,0:T(8,128)(2,1)}), bf16[4,32,640]{2,1,0:T(8,128)(2,1)S(1)}, u32[]{:S(2)}, u32[]{:S(2)}) async-start(bf16[4,32,640]{2,1,0:T(8,128)(2,1)} %broadcast_in_dim.69), calls=%async_computation.3 | async-start | bytes 327680 | tf_op jit(solution)/shard_map/all_to_all | solution.py:24
  105.3 1.4 collective-permute-done.2
  106.7 13.4 %all-to-all-done.3 = bf16[4,32,640]{2,1,0:T(8,128)(2,1)S(1)} async-done(((bf16[4,32,640]{2,1,0:T(8,128)(2,1)}), bf16[4,32,640]{2,1,0:T(8,128)(2,1)S(1)}, u32[]{:S(2)}, u32[]{:S(2)}) %all-to-all-start.3) | async-done | bytes 163872 | tf_op jit(solution)/shard_map/all_to_all | solution.py:24
  120.1 0.8 broadcast_in_dim.70
  120.9 3.5 %all-to-all-start.4 = ((bf16[8,32,640]{2,1,0:T(8,128)(2,1)}), bf16[8,32,640]{2,1,0:T(8,128)(2,1)S(1)}, u32[]{:S(2)}, u32[]{:S(2)}) async-start(bf16[8,32,640]{2,1,0:T(8,128)(2,1)} %broadcast_in_dim.70), calls=%async_computation.4 | async-start | bytes 655360 | tf_op jit(solution)/shard_map/all_to_all | solution.py:24
  124.4 10.2 %all-to-all-done.4 = bf16[8,32,640]{2,1,0:T(8,128)(2,1)S(1)} async-done(((bf16[8,32,640]{2,1,0:T(8,128)(2,1)}), bf16[8,32,640]{2,1,0:T(8,128)(2,1)S(1)}, u32[]{:S(2)}, u32[]{:S(2)}) %all-to-all-start.4) | async-done | bytes 327712 | tf_op jit(solution)/shard_map/all_to_all | solution.py:24
  134.7 2.3 %all_gather.26 = bf16[2,256,640]{2,1,0:T(8,128)(2,1)S(1)} all-gather(bf16[1,256,640]{2,1,0:T(8,128)(2,1)S(1)} %bitcast.59), channel_id=1, replica_groups=mesh['zh'=4,'zl'=4,'xl'=2,'c'=2,'xh'=2,'y'=4] {'c'}, dimensions={0}, use_global_device_ids=true | all-gather | bytes 983040 | tf_op jit(solution)/shard_map/all_gather | solution.py:103
  137.0 0.8 copy-done.4
  137.8 0.5 fusion.11
  138.2 0.3 copy-done.2
  138.5 2.5 %fusion = bf16[256,1024]{1,0:T(8,128)(2,1)} fusion(f32[256,1024]{1,0:T(8,128)S(1)} %fusion.11, bf16[1024,512]{1,0:T(8,128)(2,1)} %collective-permute-done, bf16[256,640]{1,0:T(8,128)(2,1)S(1)} %get-tuple-element.29), kind=kOutput, calls=%fused_computation.6 | convolution fusion | flops 268959744 | bytes 2883584 | tf_op jit(solution)/shard_map/dot_general | solution.py:20
  141.0 4.5 %all-to-all-start.5 = ((bf16[4,64,1024]{2,1,0:T(8,128)(2,1)}), bf16[4,64,1024]{2,1,0:T(8,128)(2,1)S(1)}, u32[]{:S(2)}, u32[]{:S(2)}) async-start(bf16[4,64,1024]{2,1,0:T(8,128)(2,1)} %bitcast.16), calls=%async_computation.5 | async-start | bytes 1048576 | tf_op jit(solution)/shard_map/all_to_all | solution.py:24
  145.5 2.5 %collective-permute-start.3 = (bf16[128,512]{1,0:T(8,128)(2,1)S(1)}, bf16[128,512]{1,0:T(8,128)(2,1)S(1)}, u32[]{:S(2)}, u32[]{:S(2)}) collective-permute-start(bf16[128,512]{1,0:T(8,128)(2,1)S(1)} %dynamic-slice_bitcast_fusion.2), channel_id=1, source_target_pairs={{0,4},{4,0},{1,5},{5,1},{2,6},{6,2},{3,7},{7,3},{8,12},{12,8},{9,1... | collective-permute-start | bytes 393224 | tf_op jit(solution)/shard_map/ppermute | solution.py:38
  148.1 1.6 convert_reduce_fusion.7
  151.0 2.9 %collective-permute-done.3 = bf16[128,512]{1,0:T(8,128)(2,1)S(1)} collective-permute-done((bf16[128,512]{1,0:T(8,128)(2,1)S(1)}, bf16[128,512]{1,0:T(8,128)(2,1)S(1)}, u32[]{:S(2)}, u32[]{:S(2)}) %collective-permute-start.3) | collective-permute-done | bytes 131104 | tf_op jit(solution)/shard_map/ppermute | solution.py:38
  153.9 0.7 copy-done.10
  154.9 1.2 broadcast_in_dim.76
  156.1 5.1 %all-to-all-start.6 = ((bf16[8,72,1024]{2,1,0:T(8,128)(2,1)}), bf16[8,72,1024]{2,1,0:T(8,128)(2,1)S(1)}, u32[]{:S(2)}, u32[]{:S(2)}) async-start(bf16[8,72,1024]{2,1,0:T(8,128)(2,1)} %broadcast_in_dim.76), calls=%async_computation.6 | async-start | bytes 2359296 | tf_op jit(solution)/shard_map/all_to_all | solution.py:24
  161.3 0.5 fusion.9
  161.7 0.4 copy-done.11
  162.1 2.0 %all_gather.27 = bf16[256,512]{1,0:T(8,128)(2,1)S(1)} all-gather(bf16[128,512]{1,0:T(8,128)(2,1)S(1)} %copy-done.11), channel_id=1, replica_groups=mesh['zh'=4,'zl'=4,'xl'=2,'c'=2,'xh'=2,'y'=4] {'c'}, dimensions={0}, use_global_device_ids=true | all-gather | bytes 393216 | tf_op jit(solution)/shard_map/all_gather | solution.py:111
  164.1 0.6 add.118
  164.7 2.5 %add_convert_fusion = bf16[1024,512]{1,0:T(8,128)(2,1)} fusion(f32[1024,512]{1,0:T(8,128)S(1)} %fusion.9, bf16[256,1024]{1,0:T(8,128)(2,1)} %collective-permute-done.2, bf16[256,512]{1,0:T(8,128)(2,1)S(1)} %all_gather.27), kind=kOutput, calls=%fused_computation.1 | convolution fusion | flops 269484032 | bytes 3932160 | tf_op jit(solution)/shard_map/dot_general | solution.py:20
  167.2 9.1 %all-to-all-done.6 = bf16[8,72,1024]{2,1,0:T(8,128)(2,1)S(1)} async-done(((bf16[8,72,1024]{2,1,0:T(8,128)(2,1)}), bf16[8,72,1024]{2,1,0:T(8,128)(2,1)S(1)}, u32[]{:S(2)}, u32[]{:S(2)}) %all-to-all-start.6) | async-done | bytes 1179680 | tf_op jit(solution)/shard_map/all_to_all | solution.py:24
  176.4 0.5 fusion.23
  176.9 0.6 slice_add_fusion
  177.6 1.7 convolution_convert_fusion
  (58 shorter events, 1.0 us)
Async XLA Ops:
  0.6 43.5 %copy-start = (bf16[512,1024]{1,0:T(8,128)(2,1)S(1)}, bf16[512,1024]{1,0:T(8,128)(2,1)}, u32[]{:S(2)}) copy-start(bf16[512,1024]{1,0:T(8,128)(2,1)} %param.8) | copy-start | bytes 3145732
  0.6 42.7 %collective-permute-start = (bf16[1024,512]{1,0:T(8,128)(2,1)}, bf16[1024,512]{1,0:T(8,128)(2,1)}, u32[]{:S(2)}, u32[]{:S(2)}) collective-permute-start(bf16[1024,512]{1,0:T(8,128)(2,1)} %param.10), channel_id=1, source_target_pairs={{0,4},{4,0},{1,5},{5,1},{2,6},{6,2},{3,7},{7,3},{8,12},{12,8},{9,1... | collective-permute-start | bytes 3145736 | tf_op jit(solution)/shard_map/ppermute | solution.py:38
  43.3 0.8 copy-start.8
  43.3 7.4 %copy-start.13 = (bf16[8,512]{1,0:T(8,128)(2,1)S(1)}, bf16[8,512]{1,0:T(8,128)(2,1)}, u32[]{:S(2)}) copy-start(bf16[8,512]{1,0:T(8,128)(2,1)} %param.7) | copy-start | bytes 24580
  43.3 7.4 %copy-start.14 = (f32[512]{0:T(512)S(1)}, f32[512]{0:T(512)}, u32[]{:S(2)}) copy-start(f32[512]{0:T(512)} %param.11) | copy-start | bytes 6148
  43.3 8.1 %copy-start.1 = (bf16[1024,512]{1,0:T(8,128)(2,1)S(1)}, bf16[1024,512]{1,0:T(8,128)(2,1)}, u32[]{:S(2)}) copy-start(bf16[1024,512]{1,0:T(8,128)(2,1)} %param.10) | copy-start | bytes 3145732
  45.8 19.8 %all-to-all-start.1 = ((bf16[8,64,1024]{2,1,0:T(8,128)(2,1)}), bf16[8,64,1024]{2,1,0:T(8,128)(2,1)S(1)}, u32[]{:S(2)}, u32[]{:S(2)}) async-start(bf16[8,64,1024]{2,1,0:T(8,128)(2,1)} %bitcast.60), calls=%async_computation.1 | async-start | bytes 2097152 | tf_op jit(solution)/shard_map/all_to_all | solution.py:24
  50.7 4.0 %collective-permute-start.1 = (f32[8,512]{1,0:T(8,128)S(1)}, f32[8,512]{1,0:T(8,128)S(1)}, u32[]{:S(2)}, u32[]{:S(2)}) collective-permute-start(f32[8,512]{1,0:T(8,128)S(1)} %convert_subtract_fusion), channel_id=1, source_target_pairs={{0,0},{4,8},{8,4},{12,12},{1,1},{5,9},{9,5},{13,13},{2,2},{6,10},{... | collective-permute-start | bytes 49160 | tf_op jit(solution)/shard_map/ppermute | solution.py:76
  51.4 14.3 %copy-start.12 = (f32[1024]{0:T(1024)S(1)}, f32[1024]{0:T(1024)}, u32[]{:S(2)}) copy-start(f32[1024]{0:T(1024)} %param.9) | copy-start | bytes 12292
  65.6 13.8 %copy-start.5 = (bf16[2,1024,512]{2,1,0:T(8,128)(2,1)S(1)}, bf16[2,1024,512]{2,1,0:T(8,128)(2,1)}, u32[]{:S(2)}) copy-start(bf16[2,1024,512]{2,1,0:T(8,128)(2,1)} %maximum_select_fusion) | copy-start | bytes 6291460
  79.4 8.6 %copy-start.6 = (bf16[256,1024]{1,0:T(8,128)(2,1)}, bf16[256,1024]{1,0:T(8,128)(2,1)S(1)}, u32[]{:S(2)}) copy-start(bf16[256,1024]{1,0:T(8,128)(2,1)S(1)} %all_gather.23) | copy-start | bytes 1572868
  83.2 14.8 %all-to-all-start.2 = ((bf16[8,32,512]{2,1,0:T(8,128)(2,1)}), bf16[8,32,512]{2,1,0:T(8,128)(2,1)S(1)}, u32[]{:S(2)}, u32[]{:S(2)}) async-start(bf16[8,32,512]{2,1,0:T(8,128)(2,1)} %bitcast.8), calls=%async_computation.2 | async-start | bytes 524288 | tf_op jit(solution)/shard_map/all_to_all | solution.py:24
  88.0 18.6 %collective-permute-start.2 = (bf16[256,1024]{1,0:T(8,128)(2,1)S(1)}, bf16[256,1024]{1,0:T(8,128)(2,1)}, u32[]{:S(2)}, u32[]{:S(2)}) collective-permute-start(bf16[256,1024]{1,0:T(8,128)(2,1)S(1)} %all_gather.23), channel_id=1, source_target_pairs={{0,4},{4,0},{1,5},{5,1},{2,6},{6,2},{3,7},{7,3},{8,12},{12,8},{9,1... | collective-permute-start | bytes 1572872 | tf_op jit(solution)/shard_map/ppermute | solution.py:38
  98.7 21.3 %all-to-all-start.3 = ((bf16[4,32,640]{2,1,0:T(8,128)(2,1)}), bf16[4,32,640]{2,1,0:T(8,128)(2,1)S(1)}, u32[]{:S(2)}, u32[]{:S(2)}) async-start(bf16[4,32,640]{2,1,0:T(8,128)(2,1)} %broadcast_in_dim.69), calls=%async_computation.3 | async-start | bytes 327680 | tf_op jit(solution)/shard_map/all_to_all | solution.py:24
  120.9 13.8 %all-to-all-start.4 = ((bf16[8,32,640]{2,1,0:T(8,128)(2,1)}), bf16[8,32,640]{2,1,0:T(8,128)(2,1)S(1)}, u32[]{:S(2)}, u32[]{:S(2)}) async-start(bf16[8,32,640]{2,1,0:T(8,128)(2,1)} %broadcast_in_dim.70), calls=%async_computation.4 | async-start | bytes 655360 | tf_op jit(solution)/shard_map/all_to_all | solution.py:24
  136.9 0.8 copy-start.4
  137.8 0.7 copy-start.2
  141.0 13.6 %all-to-all-start.5 = ((bf16[4,64,1024]{2,1,0:T(8,128)(2,1)}), bf16[4,64,1024]{2,1,0:T(8,128)(2,1)S(1)}, u32[]{:S(2)}, u32[]{:S(2)}) async-start(bf16[4,64,1024]{2,1,0:T(8,128)(2,1)} %bitcast.16), calls=%async_computation.5 | async-start | bytes 1048576 | tf_op jit(solution)/shard_map/all_to_all | solution.py:24
  145.5 8.4 %collective-permute-start.3 = (bf16[128,512]{1,0:T(8,128)(2,1)S(1)}, bf16[128,512]{1,0:T(8,128)(2,1)S(1)}, u32[]{:S(2)}, u32[]{:S(2)}) collective-permute-start(bf16[128,512]{1,0:T(8,128)(2,1)S(1)} %dynamic-slice_bitcast_fusion.2), channel_id=1, source_target_pairs={{0,4},{4,0},{1,5},{5,1},{2,6},{6,2},{3,7},{7,3},{8,12},{12,8},{9,1... | collective-permute-start | bytes 393224 | tf_op jit(solution)/shard_map/ppermute | solution.py:38
  153.9 0.7 copy-start.10
  154.7 6.5 %copy-start.3 = (bf16[256,640]{1,0:T(8,128)(2,1)S(1)}, bf16[256,640]{1,0:T(8,128)(2,1)}, u32[]{:S(2)}) copy-start(bf16[256,640]{1,0:T(8,128)(2,1)} %copy-done.2) | copy-start | bytes 983044
  154.8 6.4 %copy-start.7 = (bf16[256,1024]{1,0:T(8,128)(2,1)S(1)}, bf16[256,1024]{1,0:T(8,128)(2,1)}, u32[]{:S(2)}) copy-start(bf16[256,1024]{1,0:T(8,128)(2,1)} %copy-done.6) | copy-start | bytes 1572868
  156.1 20.3 %all-to-all-start.6 = ((bf16[8,72,1024]{2,1,0:T(8,128)(2,1)}), bf16[8,72,1024]{2,1,0:T(8,128)(2,1)S(1)}, u32[]{:S(2)}, u32[]{:S(2)}) async-start(bf16[8,72,1024]{2,1,0:T(8,128)(2,1)} %broadcast_in_dim.76), calls=%async_computation.6 | async-start | bytes 2359296 | tf_op jit(solution)/shard_map/all_to_all | solution.py:24
  161.2 0.9 copy-start.11
  176.3 1.2 copy-start.9
